TPU v7x, 32 devices: a whole 2x2x4 slice. The times are simulated.
32 devices in a mesh: wide: 16 (over z, y, x), narrow: 2 (over core).
Axes of the slice: x: 2, y: 2, z: 4, core: 2. Of those that a mesh axis runs over, the one named last changes fastest.
Arguments:
- inputs: bfloat16 [16, 1024, 768], P('wide', 'narrow'), may hold values from -6 to 6
- enc_norm_gain: bfloat16 [768], P(('wide', 'narrow')), may hold values from 0.25 to 1.75
- enc_norm_bias: bfloat16 [768], P(('wide', 'narrow')), may hold values from -3 to 3
- enc_qkv: bfloat16 [768, 2304], P(('wide', 'narrow')), may hold values from -0.21875 to 0.21875
- enc_proj: bfloat16 [768, 768], P(('wide', 'narrow')), may hold values from -1.75 to 1.75
- enc_mlp_gain: bfloat16 [768], P(('wide', 'narrow')), may hold values from 0.25 to 1.75
- enc_mlp_bias: bfloat16 [768], P(('wide', 'narrow')), may hold values from -3 to 3
- enc_up: bfloat16 [768, 3072], P(('wide', 'narrow')), may hold values from -0.21875 to 0.21875
- enc_down: bfloat16 [3072, 768], P(('wide', 'narrow')), may hold values from -0.109375 to 0.109375
- embed_weight: bfloat16 [768, 512], P(('wide', 'narrow')), may hold values from -0.21875 to 0.21875
- mask_token: bfloat16 [512], P(('wide', 'narrow')), may hold values from -4 to 4
- dec_norm_gain: bfloat16 [512], P(('wide', 'narrow')), may hold values from 0.25 to 1.75
- dec_norm_bias: bfloat16 [512], P(('wide', 'narrow')), may hold values from -3 to 3
- dec_qkv: bfloat16 [512, 1536], P(('wide', 'narrow')), may hold values from -0.25 to 0.25
- dec_proj: bfloat16 [512, 512], P(('wide', 'narrow')), may hold values from -4 to 4
- dec_mlp_gain: bfloat16 [512], P(('wide', 'narrow')), may hold values from 0.25 to 1.75
- dec_mlp_bias: bfloat16 [512], P(('wide', 'narrow')), may hold values from -3 to 3
- dec_up: bfloat16 [512, 2048], P(('wide', 'narrow')), may hold values from -0.25 to 0.25
- dec_down: bfloat16 [2048, 512], P(('wide', 'narrow')), may hold values from -0.125 to 0.125
- cotangent: bfloat16 [256, 196, 512], P(('wide', 'narrow')), may hold values from -6 to 6
- visible_counts: int32 [16, 16], P('wide'), may hold values from 1 to 128, as said below
- patch_positions: int32 [16, 1024], P('wide', 'narrow'), may hold values from 0 to 195, as said below
- image_owner: int32 [256], replicated, may hold values from 0 to 255, as said below
Outputs:
- decoded: bfloat16 [256, 196, 512], P(('wide', 'narrow'))
- grad_inputs: float32 [16, 1024, 768], P('wide', 'narrow')
- grad_enc_norm_gain: float32 [768], P(('wide', 'narrow'))
- grad_enc_norm_bias: float32 [768], P(('wide', 'narrow'))
- grad_enc_qkv: float32 [768, 2304], P(('wide', 'narrow'))
- grad_enc_proj: float32 [768, 768], P(('wide', 'narrow'))
- grad_enc_mlp_gain: float32 [768], P(('wide', 'narrow'))
- grad_enc_mlp_bias: float32 [768], P(('wide', 'narrow'))
- grad_enc_up: float32 [768, 3072], P(('wide', 'narrow'))
- grad_enc_down: float32 [3072, 768], P(('wide', 'narrow'))
- grad_embed_weight: float32 [768, 512], P(('wide', 'narrow'))
- grad_mask_token: float32 [512], P(('wide', 'narrow'))
- grad_dec_norm_gain: float32 [512], P(('wide', 'narrow'))
- grad_dec_norm_bias: float32 [512], P(('wide', 'narrow'))
- grad_dec_qkv: float32 [512, 1536], P(('wide', 'narrow'))
- grad_dec_proj: float32 [512, 512], P(('wide', 'narrow'))
- grad_dec_mlp_gain: float32 [512], P(('wide', 'narrow'))
- grad_dec_mlp_bias: float32 [512], P(('wide', 'narrow'))
- grad_dec_up: float32 [512, 2048], P(('wide', 'narrow'))
- grad_dec_down: float32 [2048, 512], P(('wide', 'narrow'))
Inputs may be any that keep to these rules, and one draw needn't show every extreme that they name: `visible_counts`: each row sums to 1024. In each row exactly one image has 128 visible patches, and it is the first or the last image of its sequence. `patch_positions`: the positions of the rows of one image are distinct. A permutation of the images: image i is decoded on device image_owner[i] // 8 of wide+narrow (wide index times 2 plus narrow index), in slot image_owner[i] % 8. The images of the sequence of wide index w are decoded by the two devices of wide index w, 8 on each.
All inputs are finite; a program needn't handle non-finite values.
Results may differ from a plain program's by a relative error of at most 0.017.
Values may be sent and summed in bfloat16 or wider, within the bound.
No kernel may reach another device: no remote copies, remote signals or barrier semaphores. Data moves between devices by JAX's collectives and lax.ppermute only.
A program may use at most 384 MiB of HBM per device.

v0:
```python
import math

import jax
import jax.numpy as jnp
from jax import lax
from jax.sharding import PartitionSpec as P

HEADS = 12
HEAD_DIM = 64
DD = 512
DHEADS = 16
DHEAD_DIM = 32
PATCHES = 196
SEQ = 1024
IMG_SEQ = 16


EPSILON = 1e-06
NEGATIVE = -1e30


def product(left_side, right_side):
    return jnp.dot(left_side, right_side, preferred_element_type=jnp.float32)


def outer_sum(left_side, right_side):
    return lax.dot_general(
        left_side, right_side, (((0,), (0,)), ((), ())), preferred_element_type=jnp.float32
    )


def back_product(grad_rows, weight):
    return lax.dot_general(
        grad_rows, weight, (((1,), (1,)), ((), ())), preferred_element_type=jnp.float32
    )


def norm_rows(values, norm_gain, norm_bias):
    center = values - jnp.mean(values, axis=-1, keepdims=True)
    scaled = center * lax.rsqrt(jnp.mean(center * center, axis=-1, keepdims=True) + EPSILON)
    return scaled * norm_gain.astype(jnp.float32) + norm_bias.astype(jnp.float32)


def exact_gelu(values):
    return jax.nn.gelu(values, approximate=False)


def position_table(model_width):
    grid_side = math.isqrt(PATCHES)
    patch_index = jnp.arange(PATCHES)
    row_coord = (patch_index // grid_side).astype(jnp.float32)[:, None]
    col_coord = (patch_index % grid_side).astype(jnp.float32)[:, None]
    quarter = model_width // 4
    frequency = jnp.power(10000.0, -jnp.arange(quarter).astype(jnp.float32) / quarter)[None, :]
    return jnp.concatenate(
        [
            jnp.sin(row_coord * frequency),
            jnp.cos(row_coord * frequency),
            jnp.sin(col_coord * frequency),
            jnp.cos(col_coord * frequency),
        ],
        axis=1,
    )


def score_rows(queries, keys_all, allowed, score_scale):
    scores = (
        jnp.einsum("bqhd,bkhd->bhqk", queries, keys_all, preferred_element_type=jnp.float32)
        * score_scale
    )
    if allowed is None:
        return scores
    return jnp.where(allowed, scores, NEGATIVE)


def attend(queries, keys_all, values_all, allowed, score_scale):
    scores = score_rows(queries, keys_all, allowed, score_scale)
    highest = jnp.max(scores, axis=-1, keepdims=True)
    raised = jnp.exp(scores - highest)
    totals = jnp.sum(raised, axis=-1, keepdims=True)
    weights = (raised / totals).astype(jnp.bfloat16)
    context = jnp.einsum("bhqk,bkhd->bqhd", weights, values_all, preferred_element_type=jnp.float32)
    return (context.astype(jnp.bfloat16), highest, totals)


def attend_back(queries, keys_all, values_all, allowed, score_scale, highest, totals, d_context):
    scores = score_rows(queries, keys_all, allowed, score_scale)
    probability = jnp.exp(scores - highest) / totals
    d_probs = jnp.einsum(
        "bqhd,bkhd->bhqk", d_context, values_all, preferred_element_type=jnp.float32
    )
    row_inner = jnp.sum(probability * d_probs, axis=-1, keepdims=True)
    d_scores = (probability * (d_probs - row_inner)).astype(jnp.bfloat16)
    d_queries = (
        jnp.einsum("bhqk,bkhd->bqhd", d_scores, keys_all, preferred_element_type=jnp.float32)
        * score_scale
    )
    d_keys = (
        jnp.einsum("bhqk,bqhd->bkhd", d_scores, queries, preferred_element_type=jnp.float32)
        * score_scale
    )
    d_values = jnp.einsum(
        "bhqk,bqhd->bkhd",
        probability.astype(jnp.bfloat16),
        d_context,
        preferred_element_type=jnp.float32,
    )
    return (d_queries, d_keys, d_values)


def block_forward(residual, params, head_count, share_keys, allowed, score_scale):
    norm_gain, norm_bias, w_qkv, w_proj, mlp_gain, mlp_bias, w_up, w_down = params
    groups, length, model_width = residual.shape
    head_dim = model_width // head_count
    resid_flat = residual.reshape(groups * length, model_width)
    normed = norm_rows(resid_flat, norm_gain, norm_bias).astype(jnp.bfloat16)
    packed = (
        product(normed, w_qkv).astype(jnp.bfloat16).reshape(groups, length, 3, head_count, head_dim)
    )
    queries = packed[:, :, 0]
    keys_all, values_all = share_keys(packed[:, :, 1], packed[:, :, 2])
    context, highest, totals = attend(queries, keys_all, values_all, allowed, score_scale)
    context_flat = context.reshape(groups * length, model_width)
    middle = resid_flat + product(context_flat, w_proj)
    normed_two = norm_rows(middle, mlp_gain, mlp_bias).astype(jnp.bfloat16)
    hidden_pre = product(normed_two, w_up)
    hidden_act = exact_gelu(hidden_pre).astype(jnp.bfloat16)
    output = middle + product(hidden_act, w_down)
    saved_state = (
        resid_flat,
        normed,
        queries,
        keys_all,
        values_all,
        highest,
        totals,
        context_flat,
        middle,
        normed_two,
        hidden_pre,
        hidden_act,
    )
    return (output, saved_state)


def block_backward(d_output, saved_state, params, unshare_keys, allowed, score_scale):
    norm_gain, norm_bias, w_qkv, w_proj, mlp_gain, mlp_bias, w_up, w_down = params
    (
        resid_flat,
        normed,
        queries,
        keys_all,
        values_all,
        highest,
        totals,
        context_flat,
        middle,
        normed_two,
        hidden_pre,
        hidden_act,
    ) = saved_state
    groups, length = (queries.shape[0], queries.shape[1])
    d_branch = d_output.astype(jnp.bfloat16)
    grad_down = outer_sum(hidden_act, d_branch)
    d_act = back_product(d_branch, w_down)
    gelu_back = jax.vjp(exact_gelu, hidden_pre)[1]
    d_pre = gelu_back(d_act)[0].astype(jnp.bfloat16)
    grad_up = outer_sum(normed_two, d_pre)
    d_normed_two = back_product(d_pre, w_up)
    mlp_back = jax.vjp(
        norm_rows, middle, mlp_gain.astype(jnp.float32), mlp_bias.astype(jnp.float32)
    )[1]
    d_mid_part, grad_mlp_gain, grad_mlp_bias = mlp_back(d_normed_two)
    d_middle = d_output + d_mid_part
    d_attn = d_middle.astype(jnp.bfloat16)
    grad_proj = outer_sum(context_flat, d_attn)
    d_context = back_product(d_attn, w_proj).astype(jnp.bfloat16).reshape(queries.shape)
    d_queries, d_keys_all, d_values_all = attend_back(
        queries, keys_all, values_all, allowed, score_scale, highest, totals, d_context
    )
    d_keys, d_values = unshare_keys(d_keys_all, d_values_all)
    d_packed = (
        jnp.stack([d_queries, d_keys, d_values], axis=2)
        .astype(jnp.bfloat16)
        .reshape(groups * length, -1)
    )
    grad_qkv = outer_sum(normed, d_packed)
    d_normed = back_product(d_packed, w_qkv)
    norm_back = jax.vjp(
        norm_rows, resid_flat, norm_gain.astype(jnp.float32), norm_bias.astype(jnp.float32)
    )[1]
    d_resid_part, grad_norm_gain, grad_norm_bias = norm_back(d_normed)
    return (
        d_middle + d_resid_part,
        (
            grad_norm_gain,
            grad_norm_bias,
            grad_qkv,
            grad_proj,
            grad_mlp_gain,
            grad_mlp_bias,
            grad_up,
            grad_down,
        ),
    )


def keep_local(first_part, second_part):
    return (first_part, second_part)


def shards(
    inputs,
    enc_norm_gain,
    enc_norm_bias,
    enc_qkv,
    enc_proj,
    enc_mlp_gain,
    enc_mlp_bias,
    enc_up,
    enc_down,
    embed_weight,
    mask_token,
    dec_norm_gain,
    dec_norm_bias,
    dec_qkv,
    dec_proj,
    dec_mlp_gain,
    dec_mlp_bias,
    dec_up,
    dec_down,
    cotangent,
    visible_counts,
    patch_positions,
    image_owner,
):
    narrow_index = lax.axis_index("narrow")
    wide_index = lax.axis_index("wide")
    half_rows = inputs.shape[1]
    narrow_count = lax.axis_size("narrow")
    slot_count = IMG_SEQ // narrow_count
    region = slot_count * PATCHES
    image_ends = jnp.cumsum(visible_counts[0], axis=0)
    position = jnp.arange(SEQ, dtype=jnp.int32)
    segment_all = jnp.sum((image_ends[None, :] <= position[:, None]).astype(jnp.int32), axis=1)
    segment_own = lax.dynamic_slice_in_dim(segment_all, narrow_index * half_rows, half_rows, 0)

    def share_sequence(keys_own, values_own):
        return (
            lax.all_gather(keys_own, "narrow", axis=1, tiled=True),
            lax.all_gather(values_own, "narrow", axis=1, tiled=True),
        )

    def unshare_sequence(d_keys_all, d_values_all):
        return (
            lax.psum_scatter(
                d_keys_all.astype(jnp.bfloat16), "narrow", scatter_dimension=1, tiled=True
            ).astype(jnp.float32),
            lax.psum_scatter(
                d_values_all.astype(jnp.bfloat16), "narrow", scatter_dimension=1, tiled=True
            ).astype(jnp.float32),
        )

    allowed = (segment_own[:, None] == segment_all[None, :])[None, None]

    def encoder_weights():
        return (
            lax.all_gather(enc_norm_gain, ("wide", "narrow"), axis=0, tiled=True),
            lax.all_gather(enc_norm_bias, ("wide", "narrow"), axis=0, tiled=True),
            lax.all_gather(enc_qkv, ("wide", "narrow"), axis=0, tiled=True),
            lax.all_gather(enc_proj, ("wide", "narrow"), axis=0, tiled=True),
            lax.all_gather(enc_mlp_gain, ("wide", "narrow"), axis=0, tiled=True),
            lax.all_gather(enc_mlp_bias, ("wide", "narrow"), axis=0, tiled=True),
            lax.all_gather(enc_up, ("wide", "narrow"), axis=0, tiled=True),
            lax.all_gather(enc_down, ("wide", "narrow"), axis=0, tiled=True),
        )

    enc_scale = HEAD_DIM ** (-0.5)
    dec_scale = DHEAD_DIM ** (-0.5)
    residual = inputs.astype(jnp.float32)
    enc_params = encoder_weights()
    encoded, enc_saved = block_forward(
        residual, enc_params, HEADS, share_sequence, allowed, enc_scale
    )
    encoded_low = encoded.astype(jnp.bfloat16)
    dec_all = (
        lax.all_gather(embed_weight, ("wide", "narrow"), axis=0, tiled=True),
        lax.all_gather(mask_token, ("wide", "narrow"), axis=0, tiled=True),
        lax.all_gather(dec_norm_gain, ("wide", "narrow"), axis=0, tiled=True),
        lax.all_gather(dec_norm_bias, ("wide", "narrow"), axis=0, tiled=True),
        lax.all_gather(dec_qkv, ("wide", "narrow"), axis=0, tiled=True),
        lax.all_gather(dec_proj, ("wide", "narrow"), axis=0, tiled=True),
        lax.all_gather(dec_mlp_gain, ("wide", "narrow"), axis=0, tiled=True),
        lax.all_gather(dec_mlp_bias, ("wide", "narrow"), axis=0, tiled=True),
        lax.all_gather(dec_up, ("wide", "narrow"), axis=0, tiled=True),
        lax.all_gather(dec_down, ("wide", "narrow"), axis=0, tiled=True),
    )
    w_embed = dec_all[0]
    mask_vector = dec_all[1].astype(jnp.float32)
    dec_params = dec_all[2:]
    embedded = product(encoded_low, w_embed).astype(jnp.bfloat16)
    image_global = wide_index * IMG_SEQ + segment_own
    owner_value = image_owner[image_global]
    destination = owner_value // slot_count - wide_index * narrow_count
    slot_index = owner_value % slot_count
    send_index = destination * half_rows + jnp.arange(half_rows, dtype=jnp.int32)
    send_rows = jnp.zeros((narrow_count * half_rows, DD), jnp.bfloat16).at[send_index].set(embedded)
    send_meta = (
        jnp.full((narrow_count * half_rows,), -1, jnp.int32)
        .at[send_index]
        .set(slot_index * PATCHES + patch_positions[0])
    )
    got_rows, got_meta = (
        lax.all_to_all(
            send_rows.reshape(narrow_count, half_rows, DD),
            "narrow",
            split_axis=0,
            concat_axis=0,
            tiled=True,
        ),
        lax.all_to_all(
            send_meta.reshape(narrow_count, half_rows),
            "narrow",
            split_axis=0,
            concat_axis=0,
            tiled=True,
        ),
    )
    meta_flat = got_meta.reshape(-1)
    target = jnp.where(meta_flat >= 0, meta_flat, region)
    placed = (
        jnp.zeros((region + 1, DD), jnp.float32)
        .at[target]
        .set(got_rows.reshape(-1, DD).astype(jnp.float32))
    )
    visible_slot = jnp.zeros((region + 1,), jnp.float32).at[target].set(1.0)[:region]
    start_rows = jnp.where(visible_slot[:, None] > 0, placed[:region], mask_vector[None, :])
    dec_input = start_rows.reshape(slot_count, PATCHES, DD) + position_table(DD)[None]
    dec_out, dec_saved = block_forward(dec_input, dec_params, DHEADS, keep_local, None, dec_scale)
    decoded = dec_out.reshape(slot_count, PATCHES, DD).astype(jnp.bfloat16)
    d_dec_out = cotangent.astype(jnp.float32).reshape(region, DD)
    d_start, dec_grads = block_backward(
        d_dec_out, dec_saved, dec_params, keep_local, None, dec_scale
    )
    grad_mask = jnp.sum(jnp.where(visible_slot[:, None] > 0, 0.0, d_start), axis=0)
    padded_grad = jnp.concatenate([d_start, jnp.zeros((1, DD), jnp.float32)], axis=0)
    d_sent = padded_grad[target].astype(jnp.bfloat16).reshape(narrow_count, half_rows, DD)
    d_back = lax.all_to_all(d_sent, "narrow", split_axis=0, concat_axis=0, tiled=True)
    d_embedded = d_back.reshape(narrow_count * half_rows, DD)[send_index]
    grad_embed = outer_sum(encoded_low, d_embedded)
    d_encoded = back_product(d_embedded, w_embed)
    enc_now = encoder_weights()
    saved_now = block_forward(residual, enc_now, HEADS, share_sequence, allowed, enc_scale)[1]
    d_inputs, enc_grads = block_backward(
        d_encoded, saved_now, enc_now, unshare_sequence, allowed, enc_scale
    )
    summed = (
        lax.psum_scatter(grad_embed, ("wide", "narrow"), scatter_dimension=0, tiled=True),
        lax.psum_scatter(grad_mask, ("wide", "narrow"), scatter_dimension=0, tiled=True),
        lax.psum_scatter(dec_grads[0], ("wide", "narrow"), scatter_dimension=0, tiled=True),
        lax.psum_scatter(dec_grads[1], ("wide", "narrow"), scatter_dimension=0, tiled=True),
        lax.psum_scatter(dec_grads[2], ("wide", "narrow"), scatter_dimension=0, tiled=True),
        lax.psum_scatter(dec_grads[3], ("wide", "narrow"), scatter_dimension=0, tiled=True),
        lax.psum_scatter(dec_grads[4], ("wide", "narrow"), scatter_dimension=0, tiled=True),
        lax.psum_scatter(dec_grads[5], ("wide", "narrow"), scatter_dimension=0, tiled=True),
        lax.psum_scatter(dec_grads[6], ("wide", "narrow"), scatter_dimension=0, tiled=True),
        lax.psum_scatter(dec_grads[7], ("wide", "narrow"), scatter_dimension=0, tiled=True),
        lax.psum_scatter(enc_grads[0], ("wide", "narrow"), scatter_dimension=0, tiled=True),
        lax.psum_scatter(enc_grads[1], ("wide", "narrow"), scatter_dimension=0, tiled=True),
        lax.psum_scatter(enc_grads[2], ("wide", "narrow"), scatter_dimension=0, tiled=True),
        lax.psum_scatter(enc_grads[3], ("wide", "narrow"), scatter_dimension=0, tiled=True),
        lax.psum_scatter(enc_grads[4], ("wide", "narrow"), scatter_dimension=0, tiled=True),
        lax.psum_scatter(enc_grads[5], ("wide", "narrow"), scatter_dimension=0, tiled=True),
        lax.psum_scatter(enc_grads[6], ("wide", "narrow"), scatter_dimension=0, tiled=True),
        lax.psum_scatter(enc_grads[7], ("wide", "narrow"), scatter_dimension=0, tiled=True),
    )
    dec_summed = summed[:10]
    enc_summed = summed[10:]
    return (decoded, d_inputs.reshape(inputs.shape)) + tuple(enc_summed) + tuple(dec_summed)


def solution(mesh):
    in_specs = (
        P("wide", "narrow", None),
        P(("wide", "narrow")),
        P(("wide", "narrow")),
        P(("wide", "narrow"), None),
        P(("wide", "narrow"), None),
        P(("wide", "narrow")),
        P(("wide", "narrow")),
        P(("wide", "narrow"), None),
        P(("wide", "narrow"), None),
        P(("wide", "narrow"), None),
        P(("wide", "narrow")),
        P(("wide", "narrow")),
        P(("wide", "narrow")),
        P(("wide", "narrow"), None),
        P(("wide", "narrow"), None),
        P(("wide", "narrow")),
        P(("wide", "narrow")),
        P(("wide", "narrow"), None),
        P(("wide", "narrow"), None),
        P(("wide", "narrow"), None, None),
        P("wide", None),
        P("wide", "narrow"),
        P(),
    )
    out_specs = (
        P(("wide", "narrow"), None, None),
        P("wide", "narrow", None),
        P(("wide", "narrow")),
        P(("wide", "narrow")),
        P(("wide", "narrow"), None),
        P(("wide", "narrow"), None),
        P(("wide", "narrow")),
        P(("wide", "narrow")),
        P(("wide", "narrow"), None),
        P(("wide", "narrow"), None),
        P(("wide", "narrow"), None),
        P(("wide", "narrow")),
        P(("wide", "narrow")),
        P(("wide", "narrow")),
        P(("wide", "narrow"), None),
        P(("wide", "narrow"), None),
        P(("wide", "narrow")),
        P(("wide", "narrow")),
        P(("wide", "narrow"), None),
        P(("wide", "narrow"), None),
    )
    return jax.shard_map(shards, mesh=mesh, in_specs=in_specs, out_specs=out_specs, check_vma=False)
```

profile of v0, /device:TPU:0, one launch (start us, length us, event | category | flops | bytes accessed | tf_op | source)
XLA Modules:
  0.0 1856.4 jit_solution(1383744761620587088)
XLA Ops:
  15.6 42.5 %all-reduce.20 = (bf16[768]{0:T(1024)(128)(2,1)S(1)}, bf16[768]{0:T(1024)(128)(2,1)S(1)}, bf16[768]{0:T(1024)(128)(2,1)S(1)}, bf16[768]{0:T(1024)(128)(2,1)S(1)}...) all-reduce(bf16[768]{0:T(1024)(128)(2,1)S(1)} %dynamic-update-slice, ...), channel_id=1, replica_groups=mesh['wide'=16,'narrow'=2] {'wide','narrow'}, use_global_device_ids=true, to_apply=%add.2 | all-reduce | flops 5632 | bytes 22528
  61.5 12.3 all-gather.12.cloned.1.call-done
  107.0 43.5 %all_gather.85 = bf16[512,512]{1,0:T(8,128)(2,1)} all-gather(bf16[16,512]{1,0:T(8,128)(2,1)S(1)} %copy-done.60), channel_id=1, replica_groups=mesh['wide'=16,'narrow'=2] {'wide','narrow'}, dimensions={0}, use_global_device_ids=true | all-gather | bytes 540672 | tf_op jit(solution)/shard_map/all_gather | solution.py:292
  150.5 39.7 %all_gather.80 = bf16[768,512]{1,0:T(8,128)(2,1)S(1)} all-gather(bf16[24,512]{1,0:T(8,128)(2,1)S(1)} %copy-done.48), channel_id=1, replica_groups=mesh['wide'=16,'narrow'=2] {'wide','narrow'}, dimensions={0}, use_global_device_ids=true | all-gather | bytes 811008 | tf_op jit(solution)/shard_map/all_gather | solution.py:287
  202.2 11.9 fusion.69
  214.2 33.9 %fusion.142 = (f32[12,512]{1,0:T(8,128)S(1)}, f32[12,512,1024]{2,1,0:T(8,128)}) fusion(f32[12,512,1024]{2,1,0:T(8,128)} %fusion.69, pred[512,1024]{1,0:T(8,128)(4,1)} %broadcast_compare_fusion), kind=kOutput, calls=%fused_computation.249 | output fusion | flops 37749760 | bytes 50880512 | tf_op jit(solution)/shard_map/sub | solution.py:79
  248.1 11.8 fusion.80
  262.7 19.7 %multiply_convert_fusion.3 = (bf16[512,3072]{1,0:T(8,128)(2,1)}, f32[512,3072]{1,0:T(8,128)}, f32[512,3072]{1,0:T(8,128)}) fusion(bf16[768,3072]{1,0:T(8,128)(2,1)} %all-gather.16.cloned.1.call-done, f32[512,768]{1,0:T(8,128)S(1)} %get-tuple-element.161, f32[768]{0:T(1024)S(1)} %convert_element_type.244, f32[768]{0:T(1024)S(1)} %convert_element_type.243, ...), kind=kOutput, calls=%fused_computation.51 | convolution fusion | flops 2520121344 | bytes 22030336 | tf_op jit(solution)/shard_map/dot_general | solution.py:23
  282.4 12.0 all-gather.18.cloned.1.call-done
  321.3 29.7 %all-gather.20.cloned.1.call-done = bf16[512,1536]{1,0:T(8,128)(2,1)} async-done(((bf16[16,1536]{1,0:T(8,128)(2,1)}), bf16[512,1536]{1,0:T(8,128)(2,1)}) %all-gather.20.cloned.1.call-update) | async-done | bytes 1572880 | tf_op jit(solution)/shard_map/all_gather | solution.py:291
  364.8 13.8 reshape.579
  384.2 16.9 fusion.144
  401.1 12.9 convert_bitcast_fusion.2
  428.6 34.6 %multiply_convert_fusion.2 = (bf16[1568,2048]{1,0:T(8,128)(2,1)}, f32[1568,2048]{1,0:T(8,128)}, f32[1568,2048]{1,0:T(8,128)}) fusion(bf16[512,2048]{1,0:T(8,128)(2,1)} %all-gather.22.cloned.1.call-done, f32[1568,512]{1,0:T(8,128)} %copy-done.5, f32[512]{0:T(512)S(1)} %copy-done.76, f32[512]{0:T(512)S(1)} %copy-done.67, f32[1568]{0:T(1024)S(1)} %fusion.109, ...), kind=kOutput, calls=%fused_computation.24 | convolution fusion | flops 3501080576 | bytes 37437696 | tf_op jit(solution)/shard_map/dot_general | solution.py:23
  467.4 14.3 add_convert_fusion
  500.8 12.7 convert_bitcast_fusion.1
  513.6 17.8 multiply_reduce_fusion
  531.4 21.9 %multiply_convert_fusion = bf16[8,16,196,196]{2,3,1,0:T(8,128)(2,1)} fusion(f32[8,16,196,196]{2,3,1,0:T(8,128)} %get-tuple-element.170, f32[8,16,196]{2,1,0:T(8,128)S(1)} %get-tuple-element.169, f32[8,16,196,196]{2,3,1,0:T(8,128)} %get-tuple-element.164, f32[8,16,196]{2,1,0:T(8,128)S(1)} %get-tuple-element.163), kind=kLoop, calls=%fused_computation.9 | loop fusion | flops 19668992 | bytes 49373184 | tf_op jit(solution)/shard_map/convert_element_type | solution.py:93
  553.3 11.0 fusion.55
  583.0 11.6 convert_element_type.272
  649.0 11.3 fusion.77
  660.4 18.7 %multiply_reduce_fusion.1 = (f32[12,512]{1,0:T(8,128)S(1)}, f32[12,512,1024]{2,1,0:T(8,128)}) fusion(f32[12,512,1024]{2,1,0:T(8,128)} %get-tuple-element.159, f32[12,512]{1,0:T(8,128)S(1)} %copy-done.41, bf16[512,12,64]{0,2,1:T(8,128)(2,1)} %bitcast.224, bf16[1,1024,1,12,64]{1,4,3,2,0:T(8,128)(2,1)} %all-gather.26.cloned.1.call-done), kind=kOutput, calls=%fused_computation.13 | convolution fusion | flops 824174592 | bytes 52740096 | tf_op jit(solution)/shard_map/bqhd,bkhd->bhqk/dot_general | solution.py:89
  679.1 16.3 multiply_convert_fusion.1
  802.4 39.2 %all-reduce.19 = (f32[768]{0:T(1024)S(1)}, f32[768]{0:T(1024)S(1)}, f32[768]{0:T(1024)S(1)}, f32[768]{0:T(1024)S(1)}, f32[512]{0:T(512)S(1)}, /*index=5*/f32[512...) all-reduce(f32[768]{0:T(1024)S(1)} %get-tuple-element.108, ...), channel_id=6, replica_groups=mesh['wide'=16,'narrow'=2] {'wide','narrow'}, use_global_device_ids=true, to_apply=%region_31.32.clone | all-reduce | flops 5632 | bytes 45056
  851.8 99.8 %reduce-scatter.24.cloned.1.call-done = f32[24,512]{1,0:T(8,128)} async-done(((f32[768,512]{1,0:T(8,128)}), f32[24,512]{1,0:T(8,128)}) %reduce-scatter.24.cloned.1.call-update) | async-done | bytes 49168 | tf_op jit(solution)/shard_map/reduce_scatter | solution.py:358
  951.5 104.7 %reduce-scatter.18.cloned.1.call-done = f32[24,768]{1,0:T(8,128)} async-done(((f32[768,768]{1,0:T(8,128)}), f32[24,768]{1,0:T(8,128)}) %reduce-scatter.18.cloned.1.call-update) | async-done | bytes 73744 | tf_op jit(solution)/shard_map/reduce_scatter | solution.py:371
  1056.2 106.4 %reduce-scatter.26.cloned.1.call-done = f32[16,1536]{1,0:T(8,128)} async-done(((f32[512,1536]{1,0:T(8,128)}), f32[16,1536]{1,0:T(8,128)}) %reduce-scatter.26.cloned.1.call-update) | async-done | bytes 98320 | tf_op jit(solution)/shard_map/reduce_scatter | solution.py:362
  1162.6 142.8 %reduce-scatter.32.cloned.1.call-done = f32[64,512]{1,0:T(8,128)} async-done(((f32[2048,512]{1,0:T(8,128)}), f32[64,512]{1,0:T(8,128)}) %reduce-scatter.32.cloned.1.call-update) | async-done | bytes 131088 | tf_op jit(solution)/shard_map/reduce_scatter | solution.py:367
  1305.4 139.6 %reduce-scatter.30.cloned.1.call-done = f32[16,2048]{1,0:T(8,128)} async-done(((f32[512,2048]{1,0:T(8,128)}), f32[16,2048]{1,0:T(8,128)}) %reduce-scatter.30.cloned.1.call-update) | async-done | bytes 131088 | tf_op jit(solution)/shard_map/reduce_scatter | solution.py:366
  1445.0 137.7 %reduce-scatter.20.cloned.1.call-done = f32[24,3072]{1,0:T(8,128)} async-done(((f32[768,3072]{1,0:T(8,128)}), f32[24,3072]{1,0:T(8,128)}) %reduce-scatter.20.cloned.1.call-update) | async-done | bytes 294928 | tf_op jit(solution)/shard_map/reduce_scatter | solution.py:374
  1582.7 142.1 %reduce-scatter.22.cloned.1.call-done = f32[96,768]{1,0:T(8,128)} async-done(((f32[3072,768]{1,0:T(8,128)}), f32[96,768]{1,0:T(8,128)}) %reduce-scatter.22.cloned.1.call-update) | async-done | bytes 294928 | tf_op jit(solution)/shard_map/reduce_scatter | solution.py:375
  1724.8 124.5 %reduce-scatter.16.cloned.1.call-done = f32[24,2304]{1,0:T(8,128)} async-done(((f32[768,2304]{1,0:T(8,128)}), f32[24,2304]{1,0:T(8,128)}) %reduce-scatter.16.cloned.1.call-update) | async-done | bytes 221200 | tf_op jit(solution)/shard_map/reduce_scatter | solution.py:370
  (364 shorter events, 333.3 us)
Async XLA Ops:
  7.2 81.2 %copy-start = (s32[256]{0:T(256)S(1)}, s32[256]{0:T(256)}, u32[]{:S(2)}) copy-start(s32[256]{0:T(256)} %param.45) | copy-start | bytes 3076
  7.2 66.6 %all-gather.12.cloned.1.call-start = ((), (), s32[]{:S(2)}) async-start(), calls=%async_computation.14 | async-start | bytes 3649536 | tf_op jit(solution)/shard_map/all_gather | solution.py:270
  7.9 194.3 %all-gather.28.cloned.1.call-start = ((), (), s32[]{:S(2)}) async-start(), calls=%async_computation.33 | async-start | bytes 2359296 | tf_op jit(solution)/shard_map/all_gather | solution.py:250
  82.5 119.7 %copy-start.10 = (bf16[512,2304]{0,1:T(8,128)(2,1)}, bf16[512,2304]{0,1:T(8,128)(2,1)S(1)}, u32[]{:S(2)}) copy-start(bf16[512,2304]{0,1:T(8,128)(2,1)S(1)} %copy.97) | copy-start | bytes 7077892
  84.0 66.5 %copy-start.48 = (bf16[24,512]{1,0:T(8,128)(2,1)S(1)}, bf16[24,512]{1,0:T(8,128)(2,1)}, u32[]{:S(2)}) copy-start(bf16[24,512]{1,0:T(8,128)(2,1)} %param.32) | copy-start | bytes 73732
  84.0 164.1 %all-gather.26.cloned.1.call-start = ((), (), s32[]{:S(2)}) async-start(), calls=%async_computation.32 | async-start | bytes 2359296 | tf_op jit(solution)/shard_map/all_gather | solution.py:251
  84.8 175.1 %all-gather.14.cloned.1.call-start = ((), (), s32[]{:S(2)}) async-start(), calls=%async_computation.15 | async-start | bytes 1216512 | tf_op jit(solution)/shard_map/all_gather | solution.py:271
  85.3 177.4 %all-gather.16.cloned.1.call-start = ((), (), s32[]{:S(2)}) async-start(), calls=%async_computation.16 | async-start | bytes 4866048 | tf_op jit(solution)/shard_map/all_gather | solution.py:274
  85.9 208.5 %all-gather.18.cloned.1.call-start = ((), (), s32[]{:S(2)}) async-start(), calls=%async_computation.17 | async-start | bytes 4866048 | tf_op jit(solution)/shard_map/all_gather | solution.py:275
  86.5 264.5 %all-gather.20.cloned.1.call-start = ((), (), s32[]{:S(2)}) async-start(), calls=%async_computation.18 | async-start | bytes 1622016 | tf_op jit(solution)/shard_map/all_gather | solution.py:291
  87.2 341.3 %all-gather.22.cloned.1.call-start = ((), (), s32[]{:S(2)}) async-start(), calls=%async_computation.19 | async-start | bytes 2162688 | tf_op jit(solution)/shard_map/all_gather | solution.py:295
  95.0 5.8 all-to-all-start
  98.3 369.1 %all-gather.24.cloned.1.call-start = ((), (), s32[]{:S(2)}) async-start(), calls=%async_computation.20 | async-start | bytes 2162688 | tf_op jit(solution)/shard_map/all_gather | solution.py:296
  99.0 674.1 %reduce-scatter.14.cloned.1.call-start = ((), (), s32[]{:S(2)}) async-start(), calls=%async_computation.22 | async-start | bytes 2359296 | tf_op jit(solution)/shard_map/reduce_scatter | solution.py:259
  99.7 251.4 %copy-start.69 = (f32[512]{0:T(512)}, f32[512]{0:T(512)S(1)}, u32[]{:S(2)}) copy-start(f32[512]{0:T(512)S(1)} %convert_element_type.255) | copy-start | bytes 6148
  100.2 250.8 %copy-start.78 = (f32[512]{0:T(512)}, f32[512]{0:T(512)S(1)}, u32[]{:S(2)}) copy-start(f32[512]{0:T(512)S(1)} %convert_element_type.256) | copy-start | bytes 6148
  100.8 161.9 %copy-start.61 = (f32[768]{0:T(1024)}, f32[768]{0:T(1024)S(1)}, u32[]{:S(2)}) copy-start(f32[768]{0:T(1024)S(1)} %convert_element_type.243) | copy-start | bytes 9220
  100.8 161.9 %copy-start.73 = (f32[768]{0:T(1024)}, f32[768]{0:T(1024)S(1)}, u32[]{:S(2)}) copy-start(f32[768]{0:T(1024)S(1)} %convert_element_type.244) | copy-start | bytes 9220
  105.8 210.2 %copy-start.49 = (pred[1568]{0:T(1024)(128)(4,1)}, pred[1568]{0:T(1024)(128)(4,1)S(1)}, u32[]{:S(2)}) copy-start(pred[1568]{0:T(1024)(128)(4,1)S(1)} %slice_compare_fusion) | copy-start | bytes 4708
  190.2 110.1 %copy-start.24 = (bf16[768,512]{1,0:T(8,128)(2,1)}, bf16[768,512]{1,0:T(8,128)(2,1)S(1)}, u32[]{:S(2)}) copy-start(bf16[768,512]{1,0:T(8,128)(2,1)S(1)} %all_gather.80) | copy-start | bytes 2359300
  319.7 103.7 %copy-start.3 = (f32[1568,512]{1,0:T(8,128)}, f32[1568,512]{1,0:T(8,128)S(1)}, u32[]{:S(2)}) copy-start(f32[1568,512]{1,0:T(8,128)S(1)} %get-tuple-element.142) | copy-start | bytes 9633796
  660.4 112.8 %reduce-scatter.12.cloned.1.call-start = ((), (), s32[]{:S(2)}) async-start(), calls=%async_computation.21 | async-start | bytes 2359296 | tf_op jit(solution)/shard_map/reduce_scatter | solution.py:256
  704.5 147.2 %reduce-scatter.28.cloned.1.call-start = ((), (), s32[]{:S(2)}) async-start(), calls=%async_computation.29 | async-start | bytes 1081344 | tf_op jit(solution)/shard_map/reduce_scatter | solution.py:363
  708.6 242.9 %reduce-scatter.24.cloned.1.call-start = ((), (), s32[]{:S(2)}) async-start(), calls=%async_computation.27 | async-start | bytes 1622016 | tf_op jit(solution)/shard_map/reduce_scatter | solution.py:358
  712.0 344.2 %reduce-scatter.18.cloned.1.call-start = ((), (), s32[]{:S(2)}) async-start(), calls=%async_computation.24 | async-start | bytes 2433024 | tf_op jit(solution)/shard_map/reduce_scatter | solution.py:371
  716.0 446.6 %reduce-scatter.26.cloned.1.call-start = ((), (), s32[]{:S(2)}) async-start(), calls=%async_computation.28 | async-start | bytes 3244032 | tf_op jit(solution)/shard_map/reduce_scatter | solution.py:362
  724.0 581.4 %reduce-scatter.32.cloned.1.call-start = ((), (), s32[]{:S(2)}) async-start(), calls=%async_computation.31 | async-start | bytes 4325376 | tf_op jit(solution)/shard_map/reduce_scatter | solution.py:367
  733.7 711.3 %reduce-scatter.30.cloned.1.call-start = ((), (), s32[]{:S(2)}) async-start(), calls=%async_computation.30 | async-start | bytes 4325376 | tf_op jit(solution)/shard_map/reduce_scatter | solution.py:366
  744.7 838.0 %reduce-scatter.20.cloned.1.call-start = ((), (), s32[]{:S(2)}) async-start(), calls=%async_computation.25 | async-start | bytes 9732096 | tf_op jit(solution)/shard_map/reduce_scatter | solution.py:374
  754.2 970.6 %reduce-scatter.22.cloned.1.call-start = ((), (), s32[]{:S(2)}) async-start(), calls=%async_computation.26 | async-start | bytes 9732096 | tf_op jit(solution)/shard_map/reduce_scatter | solution.py:375
  763.2 1086.1 %reduce-scatter.16.cloned.1.call-start = ((), (), s32[]{:S(2)}) async-start(), calls=%async_computation.23 | async-start | bytes 7299072 | tf_op jit(solution)/shard_map/reduce_scatter | solution.py:370
  801.6 1047.7 %copy-start.1 = (s32[256]{0:T(256)S(1)}, s32[256]{0:T(256)}, u32[]{:S(2)}) copy-start(s32[256]{0:T(256)} %param.45) | copy-start | bytes 3076
  (76 other events, 792.7 us)
Sparse Core Ops, SparseCore 0:
  10.9 62.8 all-gather.11
  84.1 8.5 all-gather.27
  94.3 10.9 all-gather.25
  108.1 55.9 all-gather.13
  166.8 62.3 all-gather.15
  231.9 62.4 all-gather.17
  297.3 53.7 all-gather.19
  353.9 55.2 all-gather.21
  412.0 55.2 all-gather.23
  660.5 7.9 reduce-scatter.13
  704.6 8.2 reduce-scatter.11
  715.6 136.1 reduce-scatter.27
  858.4 93.0 reduce-scatter.23
  958.1 98.0 reduce-scatter.17
  1062.0 100.5 reduce-scatter.25
  1165.3 140.0 reduce-scatter.31
  1308.1 136.8 reduce-scatter.29
  1451.3 131.3 reduce-scatter.19
  1590.2 134.5 reduce-scatter.21
  1730.9 118.3 reduce-scatter.15
where the time goes:
time: 1870 us; the launch traced here: 1860 us
  waiting for transfers between devices  1060 us (57%)
  matrix products  347 us (19%)
  blocking collectives  176 us (9%)
  local copies, waits for them, and re-layouts  144 us (8%)
  other arithmetic  105 us (6%)
    reduce_scatter x1, waiting for transfers between devices, shards(): lax.psum_scatter(dec_grads[7], ('wide', 'narrow'), scatter_dimension=0, t...  143 us
    reduce_scatter x1, waiting for transfers between devices, shards(): lax.psum_scatter(enc_grads[7], ('wide', 'narrow'), scatter_dimension=0, t...  142 us
    reduce_scatter x1, waiting for transfers between devices, shards(): lax.psum_scatter(dec_grads[6], ('wide', 'narrow'), scatter_dimension=0, t...  140 us
    reduce_scatter x1, waiting for transfers between devices, shards(): lax.psum_scatter(enc_grads[6], ('wide', 'narrow'), scatter_dimension=0, t...  138 us
    reduce_scatter x1, waiting for transfers between devices, shards(): lax.psum_scatter(enc_grads[2], ('wide', 'narrow'), scatter_dimension=0, t...  124 us
    reduce_scatter x1, waiting for transfers between devices, shards(): lax.psum_scatter(dec_grads[2], ('wide', 'narrow'), scatter_dimension=0, t...  106 us
    reduce_scatter x1, waiting for transfers between devices, shards(): lax.psum_scatter(enc_grads[3], ('wide', 'narrow'), scatter_dimension=0, t...  105 us
    reduce_scatter x1, waiting for transfers between devices, shards(): lax.psum_scatter(grad_embed, ('wide', 'narrow'), scatter_dimension=0, til...  99.8 us
  transfers between devices with their start and end apart: 21, of which 13 were waited for; matrix products, arithmetic and copies ran while one was open for 21% of the time, Pallas kernels for 0%

commit v1 on v0

--- a/solution.py
+++ b/solution.py
@@ -207,6 +207,124 @@
 
 def keep_local(first_part, second_part):
     return (first_part, second_part)
+
+
+SWAP = [(0, 1), (1, 0)]
+GATHER_ORDERS = ((0, 2, 1), (0, 1, 2), (2, 1, 0))
+
+
+class Grid:
+    def __init__(self, wide):
+        dims, at = [1, 1, 1], 0
+        while wide > 1:
+            dims[at % 3] *= 2
+            wide //= 2
+            at += 1
+        self.dims = tuple(dims)
+        self.wide = dims[0] * dims[1] * dims[2]
+
+    def split(self, wide_index):
+        _, rows, cols = self.dims
+        return (wide_index // (rows * cols), (wide_index // cols) % rows, wide_index % cols)
+
+    def ring(self, axis):
+        size = self.dims[axis]
+        order = list(range(0, size, 2)) + list(range(size - 1, 0, -2))
+        following = {order[k]: order[(k + 1) % size] for k in range(size)}
+        pairs = []
+        for source in range(self.wide):
+            place = list(self.split(source))
+            place[axis] = following[place[axis]]
+            pairs.append((source, (place[0] * self.dims[1] + place[1]) * self.dims[2] + place[2]))
+        return pairs
+
+    def own(self, axis):
+        return self.split(lax.axis_index("wide"))[axis]
+
+    def behind(self, axis, steps):
+        size, own = self.dims[axis], self.own(axis)
+        if size == 2:
+            return (own + steps) % 2
+        place = jnp.where(own % 2 == 0, own // 2, size - 1 - own // 2)
+        place = (place - steps + size) % size
+        return jnp.where(place < size // 2, 2 * place, 2 * (size - place) - 1)
+
+
+def gather_axis(grid, block, axis):
+    size = grid.dims[axis]
+    if size == 1:
+        return block
+    shape = list(block.shape)
+    shape[axis] = size
+    whole = jnp.zeros(tuple(shape), block.dtype)
+    whole = lax.dynamic_update_slice_in_dim(whole, block, grid.own(axis), axis)
+    for step in range(1, size):
+        block = lax.ppermute(block, "wide", grid.ring(axis))
+        whole = lax.dynamic_update_slice_in_dim(whole, block, grid.behind(axis, step), axis)
+    return whole
+
+
+def scatter_axis(grid, terms, axis):
+    size = grid.dims[axis]
+    if size == 1:
+        return terms.astype(jnp.float32)
+
+    def term(step):
+        part = lax.dynamic_slice_in_dim(terms, grid.behind(axis, step % size), 1, axis)
+        return part.astype(jnp.float32)
+
+    total = term(1)
+    for step in range(2, size + 1):
+        got = lax.ppermute(total.astype(jnp.bfloat16), "wide", grid.ring(axis))
+        total = got.astype(jnp.float32) + term(step)
+    return total
+
+
+def gather_parts(grid, parts):
+    gathered = []
+    for k, part in enumerate(parts):
+        block = part[None, None, None]
+        for axis in GATHER_ORDERS[k % 3]:
+            block = gather_axis(grid, block, axis)
+        gathered.append(block.reshape((grid.wide,) + part.shape))
+    return gathered
+
+
+def scatter_parts(grid, parts):
+    scattered = []
+    for k, part in enumerate(parts):
+        block = part.reshape(grid.dims + part.shape[1:])
+        for axis in GATHER_ORDERS[k % 3][::-1]:
+            block = scatter_axis(grid, block, axis)
+        scattered.append(block.reshape(part.shape[1:]))
+    return scattered
+
+
+def halves(array, core):
+    width = array.shape[-1] // 2
+    own = lax.dynamic_slice_in_dim(array, core * width, width, array.ndim - 1)
+    other = lax.dynamic_slice_in_dim(array, (1 - core) * width, width, array.ndim - 1)
+    return own, other
+
+
+def in_order(own, other, core, axis):
+    return jnp.where(
+        core == 0,
+        jnp.concatenate([own, other], axis=axis),
+        jnp.concatenate([other, own], axis=axis),
+    )
+
+
+def chip_rows(array, core):
+    own, other = halves(array, core)
+    return in_order(own, lax.ppermute(other, "narrow", SWAP), core, 0)
+
+
+def core_rows(array, core):
+    rows = array.shape[0] // 2
+    own = lax.dynamic_slice_in_dim(array, core * rows, rows, 0)
+    other = lax.dynamic_slice_in_dim(array, (1 - core) * rows, rows, 0)
+    return in_order(own, lax.ppermute(other, "narrow", SWAP), core, 1)
 
 
 def shards(
@@ -263,41 +381,112 @@
 
     allowed = (segment_own[:, None] == segment_all[None, :])[None, None]
 
-    def encoder_weights():
-        return (
-            lax.all_gather(enc_norm_gain, ("wide", "narrow"), axis=0, tiled=True),
-            lax.all_gather(enc_norm_bias, ("wide", "narrow"), axis=0, tiled=True),
-            lax.all_gather(enc_qkv, ("wide", "narrow"), axis=0, tiled=True),
-            lax.all_gather(enc_proj, ("wide", "narrow"), axis=0, tiled=True),
-            lax.all_gather(enc_mlp_gain, ("wide", "narrow"), axis=0, tiled=True),
-            lax.all_gather(enc_mlp_bias, ("wide", "narrow"), axis=0, tiled=True),
-            lax.all_gather(enc_up, ("wide", "narrow"), axis=0, tiled=True),
-            lax.all_gather(enc_down, ("wide", "narrow"), axis=0, tiled=True),
-        )
+    grid = Grid(lax.axis_size("wide"))
+    device_count = grid.wide * narrow_count
+    rows_e, rows_d = enc_qkv.shape[0], dec_qkv.shape[0]
+    width_e, width_d = enc_proj.shape[1], dec_proj.shape[1]
+    wide_e, wide_d = enc_up.shape[1], dec_up.shape[1]
+
+    vectors_e = jnp.stack([enc_norm_gain, enc_norm_bias, enc_mlp_gain, enc_mlp_bias], axis=1)
+    vectors_d = jnp.stack(
+        [dec_norm_gain, dec_norm_bias, dec_mlp_gain, dec_mlp_bias, mask_token], axis=1
+    )
+    vectors = jnp.concatenate(
+        [
+            jnp.pad(vectors_e, ((0, 0), (0, 124))),
+            jnp.pad(vectors_d, ((0, rows_e - rows_d), (0, 123))),
+        ],
+        axis=1,
+    )
+    down_groups = dec_down.shape[0] // rows_d
+    dec_packed = jnp.concatenate(
+        [
+            dec_qkv,
+            dec_proj,
+            dec_up,
+            dec_down.reshape(down_groups, rows_d, width_d)
+            .transpose(1, 0, 2)
+            .reshape(rows_d, down_groups * width_d),
+        ],
+        axis=1,
+    )
+    dec_whole = lax.all_gather(dec_packed, ("wide", "narrow"), axis=0, tiled=True)
+
+    enc_halves = [chip_rows(w, narrow_index) for w in (enc_qkv, enc_proj, enc_up, embed_weight, vectors)]
+    cut = enc_halves[2].shape[1] // 2
+    column_parts = [
+        enc_halves[0],
+        jnp.concatenate([enc_halves[1], enc_halves[2][:, :cut]], axis=1),
+        jnp.concatenate([enc_halves[2][:, cut:], enc_halves[3], enc_halves[4]], axis=1),
+    ]
+    down_half = chip_rows(enc_down, narrow_index)
+    third = down_half.shape[0] // 3
+    row_parts = [down_half[k * third : (k + 1) * third] for k in range(3)]
+    wide_parts = gather_parts(grid, column_parts + row_parts)
+    other_parts = [lax.ppermute(part, "narrow", SWAP) for part in wide_parts]
+    low_parts = [jnp.where(narrow_index == 0, a, b) for a, b in zip(wide_parts, other_parts)]
+    high_parts = [jnp.where(narrow_index == 0, b, a) for a, b in zip(wide_parts, other_parts)]
+
+    def both(part, start, stop):
+        return jnp.concatenate(
+            [low_parts[part][:, :, start:stop], high_parts[part][:, :, start:stop]], axis=2
+        ).reshape(device_count * rows_e, 2 * (stop - start))
+
+    half_p, half_v = width_e // 2, enc_halves[3].shape[1]
+    full_qkv = jnp.concatenate([low_parts[0], high_parts[0]], axis=2).reshape(width_e, 3 * width_e)
+    full_proj = both(1, 0, half_p)
+    full_up = jnp.concatenate(
+        [
+            low_parts[1][:, :, half_p:],
+            low_parts[2][:, :, :cut],
+            high_parts[1][:, :, half_p:],
+            high_parts[2][:, :, :cut],
+        ],
+        axis=2,
+    ).reshape(width_e, wide_e)
+    w_embed = both(2, cut, cut + half_v)
+    enc_vec = low_parts[2][:, :, cut + half_v :].reshape(width_e, 128)
+    dec_vec = (
+        high_parts[2][:, :, cut + half_v :]
+        .reshape(device_count, rows_e, 128)[:, :rows_d]
+        .reshape(width_d, 128)
+    )
+    full_down = jnp.concatenate(
+        [jnp.concatenate([a, b], axis=2) for a, b in zip(low_parts[3:], high_parts[3:])], axis=1
+    ).reshape(wide_e, width_e)
+    enc_params = (
+        enc_vec[:, 0],
+        enc_vec[:, 1],
+        full_qkv,
+        full_proj,
+        enc_vec[:, 2],
+        enc_vec[:, 3],
+        full_up,
+        full_down,
+    )
+    at_d = [0, 3 * width_d, 4 * width_d, 4 * width_d + wide_d]
+    dec_params = (
+        dec_vec[:, 0],
+        dec_vec[:, 1],
+        dec_whole[:, at_d[0] : at_d[1]],
+        dec_whole[:, at_d[1] : at_d[2]],
+        dec_vec[:, 2],
+        dec_vec[:, 3],
+        dec_whole[:, at_d[2] : at_d[3]],
+        dec_whole[:, at_d[3] :]
+        .reshape(device_count, rows_d, down_groups, width_d)
+        .transpose(0, 2, 1, 3)
+        .reshape(wide_d, width_d),
+    )
+    mask_vector = dec_vec[:, 4].astype(jnp.float32)
 
     enc_scale = HEAD_DIM ** (-0.5)
     dec_scale = DHEAD_DIM ** (-0.5)
     residual = inputs.astype(jnp.float32)
-    enc_params = encoder_weights()
     encoded, enc_saved = block_forward(
         residual, enc_params, HEADS, share_sequence, allowed, enc_scale
     )
     encoded_low = encoded.astype(jnp.bfloat16)
-    dec_all = (
-        lax.all_gather(embed_weight, ("wide", "narrow"), axis=0, tiled=True),
-        lax.all_gather(mask_token, ("wide", "narrow"), axis=0, tiled=True),
-        lax.all_gather(dec_norm_gain, ("wide", "narrow"), axis=0, tiled=True),
-        lax.all_gather(dec_norm_bias, ("wide", "narrow"), axis=0, tiled=True),
-        lax.all_gather(dec_qkv, ("wide", "narrow"), axis=0, tiled=True),
-        lax.all_gather(dec_proj, ("wide", "narrow"), axis=0, tiled=True),
-        lax.all_gather(dec_mlp_gain, ("wide", "narrow"), axis=0, tiled=True),
-        lax.all_gather(dec_mlp_bias, ("wide", "narrow"), axis=0, tiled=True),
-        lax.all_gather(dec_up, ("wide", "narrow"), axis=0, tiled=True),
-        lax.all_gather(dec_down, ("wide", "narrow"), axis=0, tiled=True),
-    )
-    w_embed = dec_all[0]
-    mask_vector = dec_all[1].astype(jnp.float32)
-    dec_params = dec_all[2:]
     embedded = product(encoded_low, w_embed).astype(jnp.bfloat16)
     image_global = wide_index * IMG_SEQ + segment_own
     owner_value = image_owner[image_global]
@@ -349,34 +538,89 @@
     d_embedded = d_back.reshape(narrow_count * half_rows, DD)[send_index]
     grad_embed = outer_sum(encoded_low, d_embedded)
     d_encoded = back_product(d_embedded, w_embed)
-    enc_now = encoder_weights()
-    saved_now = block_forward(residual, enc_now, HEADS, share_sequence, allowed, enc_scale)[1]
     d_inputs, enc_grads = block_backward(
-        d_encoded, saved_now, enc_now, unshare_sequence, allowed, enc_scale
-    )
-    summed = (
-        lax.psum_scatter(grad_embed, ("wide", "narrow"), scatter_dimension=0, tiled=True),
-        lax.psum_scatter(grad_mask, ("wide", "narrow"), scatter_dimension=0, tiled=True),
-        lax.psum_scatter(dec_grads[0], ("wide", "narrow"), scatter_dimension=0, tiled=True),
-        lax.psum_scatter(dec_grads[1], ("wide", "narrow"), scatter_dimension=0, tiled=True),
-        lax.psum_scatter(dec_grads[2], ("wide", "narrow"), scatter_dimension=0, tiled=True),
-        lax.psum_scatter(dec_grads[3], ("wide", "narrow"), scatter_dimension=0, tiled=True),
-        lax.psum_scatter(dec_grads[4], ("wide", "narrow"), scatter_dimension=0, tiled=True),
-        lax.psum_scatter(dec_grads[5], ("wide", "narrow"), scatter_dimension=0, tiled=True),
-        lax.psum_scatter(dec_grads[6], ("wide", "narrow"), scatter_dimension=0, tiled=True),
-        lax.psum_scatter(dec_grads[7], ("wide", "narrow"), scatter_dimension=0, tiled=True),
-        lax.psum_scatter(enc_grads[0], ("wide", "narrow"), scatter_dimension=0, tiled=True),
-        lax.psum_scatter(enc_grads[1], ("wide", "narrow"), scatter_dimension=0, tiled=True),
-        lax.psum_scatter(enc_grads[2], ("wide", "narrow"), scatter_dimension=0, tiled=True),
-        lax.psum_scatter(enc_grads[3], ("wide", "narrow"), scatter_dimension=0, tiled=True),
-        lax.psum_scatter(enc_grads[4], ("wide", "narrow"), scatter_dimension=0, tiled=True),
-        lax.psum_scatter(enc_grads[5], ("wide", "narrow"), scatter_dimension=0, tiled=True),
-        lax.psum_scatter(enc_grads[6], ("wide", "narrow"), scatter_dimension=0, tiled=True),
-        lax.psum_scatter(enc_grads[7], ("wide", "narrow"), scatter_dimension=0, tiled=True),
-    )
-    dec_summed = summed[:10]
-    enc_summed = summed[10:]
-    return (decoded, d_inputs.reshape(inputs.shape)) + tuple(enc_summed) + tuple(dec_summed)
+        d_encoded, enc_saved, enc_params, unshare_sequence, allowed, enc_scale
+    )
+    low = jnp.bfloat16
+
+    def chip_blocks(array):
+        own, other = halves(array, narrow_index)
+        got = lax.ppermute(other.astype(low), "narrow", SWAP)
+        total = own.astype(jnp.float32) + got.astype(jnp.float32)
+        return total.reshape(grid.wide, -1, total.shape[-1])
+
+    grad_vec_e = jnp.stack([enc_grads[0], enc_grads[1], enc_grads[4], enc_grads[5]], axis=1)
+    grad_vec_d = jnp.stack(
+        [dec_grads[0], dec_grads[1], dec_grads[4], dec_grads[5], grad_mask], axis=1
+    ).reshape(device_count, rows_d, 5)
+    grad_vec = jnp.concatenate(
+        [
+            jnp.pad(grad_vec_e, ((0, 0), (0, 124))),
+            jnp.pad(grad_vec_d, ((0, 0), (0, rows_e - rows_d), (0, 123))).reshape(width_e, 128),
+        ],
+        axis=1,
+    )
+    dec_grad_packed = jnp.concatenate(
+        [
+            dec_grads[2].astype(low),
+            dec_grads[3].astype(low),
+            dec_grads[6].astype(low),
+            dec_grads[7]
+            .astype(low)
+            .reshape(device_count, down_groups, rows_d, width_d)
+            .transpose(0, 2, 1, 3)
+            .reshape(width_d, down_groups * width_d),
+        ],
+        axis=1,
+    )
+    dec_sum = lax.psum_scatter(
+        dec_grad_packed, ("wide", "narrow"), scatter_dimension=0, tiled=True
+    ).astype(jnp.float32)
+    chip_qkv, chip_proj, chip_up, chip_embed, chip_vec, chip_down = [
+        chip_blocks(g)
+        for g in (enc_grads[2], enc_grads[3], enc_grads[6], grad_embed, grad_vec, enc_grads[7])
+    ]
+    sums = scatter_parts(
+        grid,
+        [
+            chip_qkv,
+            jnp.concatenate([chip_proj, chip_up[:, :, :cut]], axis=2),
+            jnp.concatenate([chip_up[:, :, cut:], chip_embed, chip_vec], axis=2),
+        ]
+        + [chip_down[:, k * third : (k + 1) * third] for k in range(3)],
+    )
+    out_qkv = core_rows(sums[0], narrow_index)
+    out_proj = core_rows(sums[1][:, :half_p], narrow_index)
+    out_up = core_rows(jnp.concatenate([sums[1][:, half_p:], sums[2][:, :cut]], axis=1), narrow_index)
+    out_embed = core_rows(sums[2][:, cut : cut + half_v], narrow_index)
+    out_vec = core_rows(sums[2][:, cut + half_v :], narrow_index)
+    out_down = core_rows(jnp.concatenate(sums[3:], axis=0), narrow_index)
+    out_vec_d = out_vec[:rows_d, 128:133]
+    return (
+        decoded,
+        d_inputs.reshape(inputs.shape),
+        out_vec[:, 0],
+        out_vec[:, 1],
+        out_qkv,
+        out_proj,
+        out_vec[:, 2],
+        out_vec[:, 3],
+        out_up,
+        out_down,
+        out_embed,
+        out_vec_d[:, 4],
+        out_vec_d[:, 0],
+        out_vec_d[:, 1],
+        dec_sum[:, at_d[0] : at_d[1]],
+        dec_sum[:, at_d[1] : at_d[2]],
+        out_vec_d[:, 2],
+        out_vec_d[:, 3],
+        dec_sum[:, at_d[2] : at_d[3]],
+        dec_sum[:, at_d[3] :]
+        .reshape(rows_d, down_groups, width_d)
+        .transpose(1, 0, 2)
+        .reshape(rows_d * down_groups, width_d),
+    )
 
 
 def solution(mesh):

time: 1870 us -> 970 us (0.52)
  waiting for transfers between devices: 1060 us -> 177 us
  blocking collectives: 176 us -> 11.6 us
  starting transfers between devices: 4.6 us -> 117 us
  matrix products: 347 us -> 304 us
  other arithmetic: 105 us -> 147 us
  local copies, waits for them, and re-layouts: 144 us -> 185 us
    reduce_scatter x9 -> x1, waiting for transfers between devices: 999 us -> 0.01 us  [shards(): lax.psum_scatter(dec_grad_packed, ('wide', 'narrow'), scatter_dimension=0...]
    ppermute x0 -> x84, waiting for transfers between devices: none -> 177 us  [the longest x30 108 us: scatter_axis(): got = lax.ppermute(total.astype(jnp.bfloat16), 'wide', grid.ring(axis))]
    ppermute x0 -> x84, starting transfers between devices: none -> 114 us  [the longest x30 65.3 us: gather_axis(): block = lax.ppermute(block, 'wide', grid.ring(axis))]
    all_gather x2 -> x0, blocking collectives: 83.2 us -> none  [the longest x1 43.5 us: shards(): lax.all_gather(dec_proj, ('wide', 'narrow'), axis=0, tiled=True)]
    unnamed x2 -> x0, blocking collectives: 81.7 us -> none
    all_gather x7 -> x1, waiting for transfers between devices: 58.2 us -> 0.01 us  [shards(): lax.all_gather(dec_packed, ('wide', 'narrow'), axis=0, tiled=True)]
    dot_general x9, matrix products: 60.2 us -> 36.7 us  [outer_sum(): lax.dot_general(left_side, right_side, (((0,), (0,)), ((), ())), preferre...]
    unnamed x203 -> x246, local copies, waits for them, and re-layouts: 37.7 us -> 26 us
  transfers between devices with their start and end apart: 21 -> 91, of which waited for: 13 -> 40; matrix products, arithmetic and copies ran while one was open for 21% -> 28% of each run, Pallas kernels for 0% -> 0%
where the time goes in v1:
time: 970 us; the launch traced here: 959 us
  matrix products  304 us (31%)
  local copies, waits for them, and re-layouts  185 us (19%)
  waiting for transfers between devices  177 us (18%)
  other arithmetic  147 us (15%)
  starting transfers between devices  117 us (12%)
  between operations  17.2 us (2%)
  blocking collectives  11.6 us (1%)
    ppermute x30, waiting for transfers between devices, scatter_axis(): got = lax.ppermute(total.astype(jnp.bfloat16), 'wide', grid.ring(axis))  108 us
    dot_general x9, matrix products, product(): return jnp.dot(left_side, right_side, preferred_element_type=jnp.float32)  73.2 us
    ppermute x30, waiting for transfers between devices, gather_axis(): block = lax.ppermute(block, 'wide', grid.ring(axis))  65.8 us
    ppermute x30, starting transfers between devices, gather_axis(): block = lax.ppermute(block, 'wide', grid.ring(axis))  65.3 us
    dot_general x9, matrix products, back_product(): lax.dot_general(grad_rows, weight, (((1,), (1,)), ((), ())), preferred_el...  49.3 us
    ppermute x30, starting transfers between devices, scatter_axis(): got = lax.ppermute(total.astype(jnp.bfloat16), 'wide', grid.ring(axis))  42.6 us
    convert_element_type x2, other arithmetic, attend_back(): d_scores = (probability * (d_probs - row_inner)).astype(jnp.bfloat16)  38.2 us
    dot_general x9, matrix products, outer_sum(): lax.dot_general(left_side, right_side, (((0,), (0,)), ((), ())), preferre...  36.7 us
  transfers between devices with their start and end apart: 91, of which 40 were waited for; matrix products, arithmetic and copies ran while one was open for 28% of the time, Pallas kernels for 0%

profile of v1, /device:TPU:0, one launch (start us, length us, event | category | flops | bytes accessed | tf_op | source)
XLA Modules:
  0.0 959.4 jit_solution(6346730840004884162)
XLA Ops:
  45.6 7.2 collective-permute-done.5
  176.7 7.6 collective-permute-done.28
  185.5 13.1 %collective-permute-done.21 = bf16[4,2,1,48,1152]{4,3,2,1,0:T(8,128)(2,1)S(1)} collective-permute-done((bf16[4,2,1,48,1152]{4,3,2,1,0:T(8,128)(2,1)S(1)}, bf16[4,2,1,48,1152]{4,3,2,1,0:T(8,128)(2,1)S(1)}, u32[]{:S(2)}, u32[]{:S(2)}) %collective-permute-start.21) | collective-permute-done | bytes 884768 | tf_op jit(solution)/shard_map/ppermute | solution.py:262
  214.2 11.5 %fusion.81 = f32[12,512,1024]{2,1,0:T(8,128)} fusion(bf16[1,1024,1,12,64]{1,4,3,2,0:T(8,128)(2,1)} %all-gather.10.cloned.1.call-done, bf16[1,512,3,12,64]{1,4,3,2,0:T(8,128)(2,1)S(1)} %bitcast.317), kind=kOutput, calls=%fused_computation.172 | convolution fusion | flops 805306368 | bytes 27525120 | tf_op jit(solution)/shard_map/bqhd,bkhd->bhqk/dot_general | solution.py:68
  225.6 34.1 %fusion.163 = (f32[12,512]{1,0:T(8,128)S(1)}, f32[12,512,1024]{2,1,0:T(8,128)}) fusion(f32[12,512,1024]{2,1,0:T(8,128)} %fusion.81, pred[512,1024]{1,0:T(8,128)(4,1)} %broadcast_compare_fusion), kind=kOutput, calls=%fused_computation.477 | output fusion | flops 37749760 | bytes 50880512 | tf_op jit(solution)/shard_map/sub | solution.py:79
  259.7 10.9 %fusion.92 = bf16[12,64,512]{2,1,0:T(8,128)(2,1)S(1)} fusion(bf16[1,1024,1,12,64]{1,4,3,2,0:T(8,128)(2,1)} %all-gather.8.cloned.1.call-done, f32[12,512,1024]{2,1,0:T(8,128)} %get-tuple-element.230, f32[12,512]{1,0:T(8,128)S(1)} %get-tuple-element.229), kind=kOutput, calls=%fused_computation.188 | convolution fusion | flops 818282496 | bytes 27549696 | tf_op jit(solution)/shard_map/bhqk,bkhd->bqhd/dot_general | solution.py:82
  272.1 18.1 %multiply_convert_fusion.3 = (bf16[512,3072]{1,0:T(8,128)(2,1)S(1)}, f32[512,3072]{1,0:T(8,128)}, f32[512,3072]{1,0:T(8,128)}) fusion(bf16[768,3072]{1,0:T(8,128)(2,1)S(1)} %bitcast.347, f32[512,768]{1,0:T(8,128)S(1)} %get-tuple-element.232, f32[768]{0:T(1024)S(1)} %copy-done.95, f32[768]{0:T(1024)S(1)} %get-tuple-element.132, f32[512]{0:T(512)S(1)} %fusion.136, ...), kind=kOutput, calls=%fused_computation.60 | convolution fusion | flops 2520121344 | bytes 22030336 | tf_op jit(solution)/shard_map/dot_general | solution.py:23
  301.7 7.2 scatter_custom_fusion.3
  331.8 7.5 copy.159
  339.3 13.8 %reshape.870 = bf16[8,196,3,16,32]{1,0,4,3,2:T(8,128)(2,1)} reshape(bf16[1568,1536]{0,1:T(8,128)(2,1)} %copy.159) | data formatting | bytes 9633792 | tf_op jit(solution)/shard_map/reshape | solution.py:118
  358.7 16.8 %fusion.165 = (f32[8,16,196]{2,1,0:T(8,128)S(1)}, f32[8,16,196,196]{2,3,1,0:T(8,128)}) fusion(bf16[8,196,1,16,32]{1,0,4,3,2:T(8,128)(2,1)} %get-tuple-element.169, bf16[8,196,1,16,32]{1,0,4,3,2:T(8,128)(2,1)} %get-tuple-element.168), kind=kOutput, calls=%fused_computation.479 | convolution fusion | flops 329455808 | bytes 22980608 | tf_op jit(solution)/shard_map/sub | solution.py:79
  375.5 12.8 %convert_bitcast_fusion.2 = bf16[8,196,16,32]{1,3,2,0:T(8,128)(2,1)} fusion(bf16[8,196,1,16,32]{1,0,4,3,2:T(8,128)(2,1)} %get-tuple-element.170, f32[8,16,196,196]{2,3,1,0:T(8,128)} %get-tuple-element.235, f32[8,16,196]{2,1,0:T(8,128)S(1)} %get-tuple-element.234), kind=kOutput, calls=%fused_computation.130 | convolution fusion | flops 325341184 | bytes 22980608 | tf_op jit(solution)/shard_map/bhqk,bkhd->bqhd/dot_general | solution.py:82
  401.6 34.1 %multiply_convert_fusion.2 = (bf16[1568,2048]{1,0:T(8,128)(2,1)S(1)}, f32[1568,2048]{1,0:T(8,128)}, f32[1568,2048]{1,0:T(8,128)}) fusion(bf16[512,6144]{1,0:T(8,128)(2,1)} %all-gather.6.cloned.1.call-done, f32[1568,512]{1,0:T(8,128)S(1)} %get-tuple-element.237, f32[512]{0:T(512)S(1)} %copy-done.97, f32[512]{0:T(512)S(1)} %copy-done.89, ...), kind=kOutput, calls=%fused_computation.32 | convolution fusion | flops 3501080576 | bytes 37437696 | tf_op jit(solution)/shard_map/dot_general | solution.py:23
  445.5 13.8 %fusion.13 = bf16[1568,2048]{1,0:T(8,128)(2,1)} fusion(f32[1568,2048]{1,0:T(8,128)} %get-tuple-element.159, f32[1568,2048]{1,0:T(8,128)} %get-tuple-element.238, bf16[2048,512]{1,0:T(8,128)(2,1)S(1)} %bitcast.369, bf16[1568,512]{1,0:T(8,128)(2,1)S(1)} %copy-done.10), kind=kOutput, calls=%fused_computation.30 | convolution fusion | flops 3333292032 | bytes 35815424 | tf_op jit(solution)/shard_map/dot_general | solution.py:33
  459.3 8.7 multiply_reduce_fusion.3
  482.2 12.7 %convert_bitcast_fusion.1 = bf16[8,196,1,16,32]{1,4,3,0,2:T(8,128)(2,1)} fusion(bf16[8,196,16,32]{1,0,3,2:T(8,128)(2,1)} %reshape.876, f32[8,16,196,196]{2,3,1,0:T(8,128)} %get-tuple-element.235, f32[8,16,196]{2,1,0:T(8,128)S(1)} %copy-done.53), kind=kOutput, calls=%fused_computation.129 | convolution fusion | flops 325341184 | bytes 22980608 | tf_op jit(solution)/shard_map/bhqk,bqhd->bkhd/dot_general | solution.py:102
  494.9 17.7 %multiply_reduce_fusion = (f32[8,16,196]{2,1,0:T(8,128)S(1)}, f32[8,16,196,196]{2,3,1,0:T(8,128)}) fusion(f32[8,16,196,196]{2,3,1,0:T(8,128)} %get-tuple-element.235, f32[8,16,196]{2,1,0:T(8,128)S(1)} %copy-done.53, bf16[8,196,1,16,32]{1,0,4,3,2:T(8,128)(2,1)} %get-tuple-element.170, bf16[8,196,16,32]{1,0,3,2:T(8,128)(2,1)S(1)} %copy-done.42), kind=kOutput, calls=%fused_computation.10 | convolution fusion | flops 329430528 | bytes 42749952 | tf_op jit(solution)/shard_map/bqhd,bkhd->bhqk/dot_general | solution.py:89
  512.6 21.9 %multiply_convert_fusion = bf16[8,16,196,196]{2,3,1,0:T(8,128)(2,1)} fusion(f32[8,16,196,196]{2,3,1,0:T(8,128)} %get-tuple-element.241, f32[8,16,196]{2,1,0:T(8,128)S(1)} %get-tuple-element.240, f32[8,16,196,196]{2,3,1,0:T(8,128)} %get-tuple-element.235, f32[8,16,196]{2,1,0:T(8,128)S(1)} %copy-done.53), kind=kLoop, calls=%fused_computation.9 | loop fusion | flops 19668992 | bytes 49373184 | tf_op jit(solution)/shard_map/convert_element_type | solution.py:93
  534.5 10.9 %fusion.68 = bf16[8,196,1,16,32]{1,4,3,0,2:T(8,128)(2,1)} fusion(bf16[8,16,196,196]{2,3,1,0:T(8,128)(2,1)} %multiply_convert_fusion, bf16[8,196,1,16,32]{1,0,4,3,2:T(8,128)(2,1)} %get-tuple-element.169), kind=kOutput, calls=%fused_computation.159 | convolution fusion | flops 316309504 | bytes 13045760 | tf_op jit(solution)/shard_map/bhqk,bqhd->bkhd/dot_general | solution.py:99
  553.6 10.4 %copy.173 = bf16[8,196,3,16,32]{1,0,4,3,2:T(8,128)(2,1)} copy(bf16[8,196,3,16,32]{1,4,3,0,2:T(8,128)(2,1)S(1)} %pad_maximum_fusion) | data formatting | bytes 9633792 | tf_op jit(solution)/shard_map/stack | solution.py:183
  564.0 11.6 %convert_element_type.575 = bf16[1568,1536]{0,1:T(8,128)(2,1)} reshape(bf16[8,196,3,16,32]{1,0,4,3,2:T(8,128)(2,1)} %copy.173) | data formatting | bytes 9633792 | tf_op jit(solution)/shard_map/convert_element_type | solution.py:184
  575.6 7.4 multiply_reduce_fusion.4
  594.8 7.0 all_to_all.20
  610.9 8.3 add_convert_fusion
  657.7 11.2 %fusion.89 = bf16[1,1024,12,64]{1,3,2,0:T(8,128)(2,1)} fusion(bf16[512,12,64]{0,2,1:T(8,128)(2,1)} %bitcast.378, f32[12,512,1024]{2,1,0:T(8,128)} %get-tuple-element.230, f32[12,512]{1,0:T(8,128)S(1)} %copy-done.66), kind=kOutput, calls=%fused_computation.186 | convolution fusion | flops 818675712 | bytes 27549696 | tf_op jit(solution)/shard_map/bhqk,bqhd->bkhd/dot_general | solution.py:102
  668.9 19.0 %multiply_reduce_fusion.1 = (f32[12,512]{1,0:T(8,128)S(1)}, f32[12,512,1024]{2,1,0:T(8,128)}) fusion(f32[12,512,1024]{2,1,0:T(8,128)} %get-tuple-element.230, f32[12,512]{1,0:T(8,128)S(1)} %copy-done.66, bf16[512,12,64]{0,2,1:T(8,128)(2,1)} %bitcast.379, bf16[1,1024,1,12,64]{1,4,3,2,0:T(8,128)(2,1)} %all-gather.8.cloned.1.call-done), kind=kOutput, calls=%fused_computation.13 | convolution fusion | flops 824174592 | bytes 52740096 | tf_op jit(solution)/shard_map/bqhd,bkhd->bhqk/dot_general | solution.py:89
  687.9 16.3 %multiply_convert_fusion.1 = bf16[12,512,1024]{2,1,0:T(8,128)(2,1)S(1)} fusion(f32[12,512,1024]{2,1,0:T(8,128)} %get-tuple-element.245, f32[12,512]{1,0:T(8,128)S(1)} %get-tuple-element.244, f32[12,512,1024]{2,1,0:T(8,128)} %get-tuple-element.230, f32[12,512]{1,0:T(8,128)S(1)} %copy-done.66), kind=kLoop, calls=%fused_computation.12 | loop fusion | flops 25165824 | bytes 62963712 | tf_op jit(solution)/shard_map/convert_element_type | solution.py:93
  739.5 9.5 fusion.100
  787.3 23.4 %collective-permute-done.68 = bf16[4,1,1,64,384]{4,3,2,1,0:T(8,128)(2,1)S(1)} collective-permute-done((bf16[4,1,1,64,384]{4,3,2,1,0:T(8,128)(2,1)S(1)}, bf16[4,1,1,64,384]{4,3,2,1,0:T(8,128)(2,1)S(1)}, u32[]{:S(2)}, u32[]{:S(2)}) %collective-permute-start.68) | collective-permute-done | bytes 196640 | tf_op jit(solution)/shard_map/ppermute | solution.py:278
  871.5 9.8 %collective-permute-done.46 = bf16[1,2,2,48,1152]{4,3,2,1,0:T(8,128)(2,1)S(1)} collective-permute-done((bf16[1,2,2,48,1152]{4,3,2,1,0:T(8,128)(2,1)S(1)}, bf16[1,2,2,48,1152]{4,3,2,1,0:T(8,128)(2,1)S(1)}, u32[]{:S(2)}, u32[]{:S(2)}) %collective-permute-start.46) | collective-permute-done | bytes 442400 | tf_op jit(solution)/shard_map/ppermute | solution.py:278
  884.6 8.6 collective-permute-done.47
  908.2 11.3 %collective-permute-done.52 = bf16[4,1,2,48,1152]{4,3,2,1,0:T(8,128)(2,1)S(1)} collective-permute-done((bf16[4,1,2,48,1152]{4,3,2,1,0:T(8,128)(2,1)S(1)}, bf16[4,1,2,48,1152]{4,3,2,1,0:T(8,128)(2,1)S(1)}, u32[]{:S(2)}, u32[]{:S(2)}) %collective-permute-start.52) | collective-permute-done | bytes 884768 | tf_op jit(solution)/shard_map/ppermute | solution.py:278
  (744 shorter events, 508.2 us)
Async XLA Ops:
  7.2 206.9 %all-gather.10.cloned.1.call-start = ((), (), s32[]{:S(2)}) async-start(), calls=%async_computation.11 | async-start | bytes 2359296 | tf_op jit(solution)/shard_map/all_gather | solution.py:368
  17.0 15.6 %collective-permute-start.3 = (bf16[1,1,1,48,1152]{4,3,2,1,0:T(8,128)(2,1)S(1)}, bf16[1,1,1,48,1152]{4,3,2,1,0:T(8,128)(2,1)S(1)}, u32[]{:S(2)}, u32[]{:S(2)}) collective-permute-start(bf16[1,1,1,48,1152]{4,3,2,1,0:T(8,128)(2,1)S(1)} %maximum_bitcast_fusion), channel_id=1, source_target_pairs={{0,2},{2,0},{4,6},{6,4},{8,10},{10,8},{12,14},{14,12},{16,18},{18,... | collective-permute-start | bytes 331784 | tf_op jit(solution)/shard_map/ppermute | solution.py:262
  40.6 18.1 %collective-permute-start.14 = (bf16[4,1,2,48,1152]{4,3,2,1,0:T(8,128)(2,1)S(1)}, bf16[4,1,2,48,1152]{4,3,2,1,0:T(8,128)(2,1)S(1)}, u32[]{:S(2)}, u32[]{:S(2)}) collective-permute-start(bf16[4,1,2,48,1152]{4,3,2,1,0:T(8,128)(2,1)S(1)} %constant_dynamic-update-slice_fusion.34), channel_id=1, source_target_pairs={{0,4},{2,6},{4,0},{6,2},{8,12},{10,14},{12,8},{14,10},{16,20},{18,... | collective-permute-start | bytes 2654216 | tf_op jit(solution)/shard_map/ppermute | solution.py:262
  87.2 172.6 %all-gather.8.cloned.1.call-start = ((), (), s32[]{:S(2)}) async-start(), calls=%async_computation.10 | async-start | bytes 2359296 | tf_op jit(solution)/shard_map/all_gather | solution.py:369
  97.8 216.4 %all-gather.6.cloned.1.call-start = ((), (), s32[]{:S(2)}) async-start(), calls=%async_computation.6 | async-start | bytes 6488064 | tf_op jit(solution)/shard_map/all_gather | solution.py:413
  98.5 23.1 %collective-permute-start.16 = (bf16[24,384]{1,0:T(8,128)(2,1)}, bf16[24,384]{1,0:T(8,128)(2,1)}, u32[]{:S(2)}, u32[]{:S(2)}) collective-permute-start(bf16[24,384]{1,0:T(8,128)(2,1)} %get-tuple-element.216), channel_id=1, source_target_pairs={{0,1},{1,0},{2,3},{3,2},{4,5},{5,4},{6,7},{7,6},{8,9},{9,8},{10,11... | collective-permute-start | bytes 55304 | tf_op jit(solution)/shard_map/ppermute | solution.py:320
  99.0 27.0 %collective-permute-start.23 = (bf16[96,384]{1,0:T(8,128)(2,1)S(1)}, bf16[96,384]{1,0:T(8,128)(2,1)S(1)}, u32[]{:S(2)}, u32[]{:S(2)}) collective-permute-start(bf16[96,384]{1,0:T(8,128)(2,1)S(1)} %get-tuple-element.204), channel_id=1, source_target_pairs={{0,1},{1,0},{2,3},{3,2},{4,5},{5,4},{6,7},{7,6},{8,9},{9,8},{10,11... | collective-permute-start | bytes 221192 | tf_op jit(solution)/shard_map/ppermute | solution.py:320
  101.5 728.0 %reduce-scatter.6.cloned.1.call-start = ((), (), s32[]{:S(2)}) async-start(), calls=%async_computation.8 | async-start | bytes 2359296 | tf_op jit(solution)/shard_map/reduce_scatter | solution.py:377
  122.5 17.8 %collective-permute-start.17 = (bf16[1,1,1,48,1152]{4,3,2,1,0:T(8,128)(2,1)S(1)}, bf16[1,1,1,48,1152]{4,3,2,1,0:T(8,128)(2,1)S(1)}, u32[]{:S(2)}, u32[]{:S(2)}) collective-permute-start(bf16[1,1,1,48,1152]{4,3,2,1,0:T(8,128)(2,1)S(1)} %maximum_bitcast_fusion.1), channel_id=1, source_target_pairs={{0,16},{2,18},{4,20},{6,22},{8,0},{10,2},{12,4},{14,6},{16,24},{18... | collective-permute-start | bytes 331784 | tf_op jit(solution)/shard_map/ppermute | solution.py:262
  143.3 19.4 %collective-permute-start.38 = (bf16[1,2,2,64,384]{4,3,2,1,0:T(8,128)(2,1)S(1)}, bf16[1,2,2,64,384]{4,3,2,1,0:T(8,128)(2,1)S(1)}, u32[]{:S(2)}, u32[]{:S(2)}) collective-permute-start(bf16[1,2,2,64,384]{4,3,2,1,0:T(8,128)(2,1)S(1)} %constant_dynamic-update-slice_fusion.4), channel_id=1, source_target_pairs={{0,16},{2,18},{4,20},{6,22},{8,0},{10,2},{12,4},{14,6},{16,24},{18... | collective-permute-start | bytes 589832 | tf_op jit(solution)/shard_map/ppermute | solution.py:262
  156.4 15.2 %collective-permute-start.20 = (bf16[4,1,1,48,1152]{4,3,2,1,0:T(8,128)(2,1)S(1)}, bf16[4,1,1,48,1152]{4,3,2,1,0:T(8,128)(2,1)S(1)}, u32[]{:S(2)}, u32[]{:S(2)}) collective-permute-start(bf16[4,1,1,48,1152]{4,3,2,1,0:T(8,128)(2,1)S(1)} %constant_dynamic-update-slice_fusion.28), channel_id=1, source_target_pairs={{0,4},{2,6},{4,0},{6,2},{8,12},{10,14},{12,8},{14,10},{16,20},{18,... | collective-permute-start | bytes 1327112 | tf_op jit(solution)/shard_map/ppermute | solution.py:262
  159.1 25.2 %collective-permute-start.28 = (bf16[4,1,2,64,384]{4,3,2,1,0:T(8,128)(2,1)S(1)}, bf16[4,1,2,64,384]{4,3,2,1,0:T(8,128)(2,1)S(1)}, u32[]{:S(2)}, u32[]{:S(2)}) collective-permute-start(bf16[4,1,2,64,384]{4,3,2,1,0:T(8,128)(2,1)S(1)} %constant_dynamic-update-slice_fusion.18), channel_id=1, source_target_pairs={{0,4},{2,6},{4,0},{6,2},{8,12},{10,14},{12,8},{14,10},{16,20},{18,... | collective-permute-start | bytes 1179656 | tf_op jit(solution)/shard_map/ppermute | solution.py:262
  159.2 25.9 %collective-permute-start.34 = (bf16[4,2,1,64,384]{4,3,2,1,0:T(8,128)(2,1)S(1)}, bf16[4,2,1,64,384]{4,3,2,1,0:T(8,128)(2,1)S(1)}, u32[]{:S(2)}, u32[]{:S(2)}) collective-permute-start(bf16[4,2,1,64,384]{4,3,2,1,0:T(8,128)(2,1)S(1)} %constant_dynamic-update-slice_fusion.10), channel_id=1, source_target_pairs={{0,2},{2,0},{4,6},{6,4},{8,10},{10,8},{12,14},{14,12},{16,18},{18,... | collective-permute-start | bytes 1179656 | tf_op jit(solution)/shard_map/ppermute | solution.py:262
  171.6 27.1 %collective-permute-start.21 = (bf16[4,2,1,48,1152]{4,3,2,1,0:T(8,128)(2,1)S(1)}, bf16[4,2,1,48,1152]{4,3,2,1,0:T(8,128)(2,1)S(1)}, u32[]{:S(2)}, u32[]{:S(2)}) collective-permute-start(bf16[4,2,1,48,1152]{4,3,2,1,0:T(8,128)(2,1)S(1)} %constant_dynamic-update-slice_fusion.26), channel_id=1, source_target_pairs={{0,2},{2,0},{4,6},{6,4},{8,10},{10,8},{12,14},{14,12},{16,18},{18,... | collective-permute-start | bytes 2654216 | tf_op jit(solution)/shard_map/ppermute | solution.py:262
  184.4 15.0 %collective-permute-start.29 = (bf16[16,64,384]{2,1,0:T(8,128)(2,1)S(1)}, bf16[16,64,384]{2,1,0:T(8,128)(2,1)S(1)}, u32[]{:S(2)}, u32[]{:S(2)}) collective-permute-start(bf16[16,64,384]{2,1,0:T(8,128)(2,1)S(1)} %bitcast.363), channel_id=1, source_target_pairs={{0,1},{1,0},{2,3},{3,2},{4,5},{5,4},{6,7},{7,6},{8,9},{9,8},{10,11... | collective-permute-start | bytes 2359304 | tf_op jit(solution)/shard_map/ppermute | solution.py:426
  184.5 15.2 %collective-permute-start.41 = (bf16[16,64,384]{2,1,0:T(8,128)(2,1)S(1)}, bf16[16,64,384]{2,1,0:T(8,128)(2,1)S(1)}, u32[]{:S(2)}, u32[]{:S(2)}) collective-permute-start(bf16[16,64,384]{2,1,0:T(8,128)(2,1)S(1)} %bitcast.362), channel_id=1, source_target_pairs={{0,1},{1,0},{2,3},{3,2},{4,5},{5,4},{6,7},{7,6},{8,9},{9,8},{10,11... | collective-permute-start | bytes 2359304 | tf_op jit(solution)/shard_map/ppermute | solution.py:426
  654.9 95.0 %collective-permute-start.43 = (bf16[768,256]{1,0:T(8,128)(2,1)}, bf16[768,256]{1,0:T(8,128)(2,1)}, u32[]{:S(2)}, u32[]{:S(2)}) collective-permute-start(bf16[768,256]{1,0:T(8,128)(2,1)} %dynamic-slice_convert_fusion.10), channel_id=1, source_target_pairs={{0,1},{1,0},{2,3},{3,2},{4,5},{5,4},{6,7},{7,6},{8,9},{9,8},{10,11... | collective-permute-start | bytes 1179656 | tf_op jit(solution)/shard_map/ppermute | solution.py:548
  657.3 94.9 %collective-permute-start.58 = (bf16[768,384]{1,0:T(8,128)(2,1)}, bf16[768,384]{1,0:T(8,128)(2,1)}, u32[]{:S(2)}, u32[]{:S(2)}) collective-permute-start(bf16[768,384]{1,0:T(8,128)(2,1)} %dynamic-slice_convert_fusion.4), channel_id=1, source_target_pairs={{0,1},{1,0},{2,3},{3,2},{4,5},{5,4},{6,7},{7,6},{8,9},{9,8},{10,11... | collective-permute-start | bytes 1769480 | tf_op jit(solution)/shard_map/ppermute | solution.py:548
  668.9 160.6 %reduce-scatter.4.cloned.1.call-start = ((), (), s32[]{:S(2)}) async-start(), calls=%async_computation.7 | async-start | bytes 2359296 | tf_op jit(solution)/shard_map/reduce_scatter | solution.py:374
  713.4 233.9 %reduce-scatter.8.cloned.1.call-start = ((), (), s32[]{:S(2)}) async-start(), calls=%async_computation.9 | async-start | bytes 6488064 | tf_op jit(solution)/shard_map/reduce_scatter | solution.py:576
  717.7 42.9 %collective-permute-start.42 = (bf16[768,1536]{1,0:T(8,128)(2,1)}, bf16[768,1536]{1,0:T(8,128)(2,1)}, u32[]{:S(2)}, u32[]{:S(2)}) collective-permute-start(bf16[768,1536]{1,0:T(8,128)(2,1)} %dynamic-slice_convert_fusion.1), channel_id=1, source_target_pairs={{0,1},{1,0},{2,3},{3,2},{4,5},{5,4},{6,7},{7,6},{8,9},{9,8},{10,11... | collective-permute-start | bytes 7077896 | tf_op jit(solution)/shard_map/ppermute | solution.py:548
  722.5 30.9 %collective-permute-start.66 = (bf16[3072,384]{1,0:T(8,128)(2,1)}, bf16[3072,384]{1,0:T(8,128)(2,1)}, u32[]{:S(2)}, u32[]{:S(2)}) collective-permute-start(bf16[3072,384]{1,0:T(8,128)(2,1)} %dynamic-slice_convert_fusion), channel_id=1, source_target_pairs={{0,1},{1,0},{2,3},{3,2},{4,5},{5,4},{6,7},{7,6},{8,9},{9,8},{10,11... | collective-permute-start | bytes 7077896 | tf_op jit(solution)/shard_map/ppermute | solution.py:548
  769.6 73.5 %collective-permute-start.59 = (bf16[4,2,1,48,1152]{4,3,2,1,0:T(8,128)(2,1)}, bf16[4,2,1,48,1152]{4,3,2,1,0:T(8,128)(2,1)}, u32[]{:S(2)}, u32[]{:S(2)}) collective-permute-start(bf16[4,2,1,48,1152]{4,3,2,1,0:T(8,128)(2,1)} %fusion.63), channel_id=1, source_target_pairs={{0,2},{2,0},{4,6},{6,4},{8,10},{10,8},{12,14},{14,12},{16,18},{18,... | collective-permute-start | bytes 2654216 | tf_op jit(solution)/shard_map/ppermute | solution.py:278
  782.8 27.9 %collective-permute-start.68 = (bf16[4,1,1,64,384]{4,3,2,1,0:T(8,128)(2,1)S(1)}, bf16[4,1,1,64,384]{4,3,2,1,0:T(8,128)(2,1)S(1)}, u32[]{:S(2)}, u32[]{:S(2)}) collective-permute-start(bf16[4,1,1,64,384]{4,3,2,1,0:T(8,128)(2,1)S(1)} %dynamic-slice_convert_fusion.14), channel_id=1, source_target_pairs={{0,2},{2,0},{4,6},{6,4},{8,10},{10,8},{12,14},{14,12},{16,18},{18,... | collective-permute-start | bytes 589832 | tf_op jit(solution)/shard_map/ppermute | solution.py:278
  783.2 34.8 %collective-permute-start.80 = (bf16[1,1,2,64,384]{4,3,2,1,0:T(8,128)(2,1)S(1)}, bf16[1,1,2,64,384]{4,3,2,1,0:T(8,128)(2,1)S(1)}, u32[]{:S(2)}, u32[]{:S(2)}) collective-permute-start(bf16[1,1,2,64,384]{4,3,2,1,0:T(8,128)(2,1)S(1)} %dynamic-slice_convert_fusion.18), channel_id=1, source_target_pairs={{0,4},{2,6},{4,0},{6,2},{8,12},{10,14},{12,8},{14,10},{16,20},{18,... | collective-permute-start | bytes 294920 | tf_op jit(solution)/shard_map/ppermute | solution.py:278
  786.0 25.8 %collective-permute-start.74 = (bf16[1,1,1,64,384]{4,3,2,1,0:T(8,128)(2,1)S(1)}, bf16[1,1,1,64,384]{4,3,2,1,0:T(8,128)(2,1)S(1)}, u32[]{:S(2)}, u32[]{:S(2)}) collective-permute-start(bf16[1,1,1,64,384]{4,3,2,1,0:T(8,128)(2,1)S(1)} %dynamic-slice_convert_fusion.20), channel_id=1, source_target_pairs={{0,16},{2,18},{4,20},{6,22},{8,0},{10,2},{12,4},{14,6},{16,24},{18... | collective-permute-start | bytes 147464 | tf_op jit(solution)/shard_map/ppermute | solution.py:278
  829.5 18.4 %collective-permute-start.82 = (f32[96,384]{1,0:T(8,128)}, f32[96,384]{1,0:T(8,128)}, u32[]{:S(2)}, u32[]{:S(2)}) collective-permute-start(f32[96,384]{1,0:T(8,128)} %get-tuple-element.191), channel_id=1, source_target_pairs={{0,1},{1,0},{2,3},{3,2},{4,5},{5,4},{6,7},{7,6},{8,9},{9,8},{10,11... | collective-permute-start | bytes 442376 | tf_op jit(solution)/shard_map/ppermute | solution.py:327
  840.8 58.5 %collective-permute-start.51 = (bf16[768,1152]{1,0:T(8,128)(2,1)}, bf16[768,1152]{1,0:T(8,128)(2,1)}, u32[]{:S(2)}, u32[]{:S(2)}) collective-permute-start(bf16[768,1152]{1,0:T(8,128)(2,1)} %dynamic-slice_convert_fusion.2), channel_id=1, source_target_pairs={{0,1},{1,0},{2,3},{3,2},{4,5},{5,4},{6,7},{7,6},{8,9},{9,8},{10,11... | collective-permute-start | bytes 5308424 | tf_op jit(solution)/shard_map/ppermute | solution.py:548
  852.1 16.0 %collective-permute-start.45 = (bf16[1,2,2,48,1152]{4,3,2,1,0:T(8,128)(2,1)S(1)}, bf16[1,2,2,48,1152]{4,3,2,1,0:T(8,128)(2,1)S(1)}, u32[]{:S(2)}, u32[]{:S(2)}) collective-permute-start(bf16[1,2,2,48,1152]{4,3,2,1,0:T(8,128)(2,1)S(1)} %dynamic-slice_convert_fusion.7), channel_id=1, source_target_pairs={{0,16},{2,18},{4,20},{6,22},{8,0},{10,2},{12,4},{14,6},{16,24},{18... | collective-permute-start | bytes 1327112 | tf_op jit(solution)/shard_map/ppermute | solution.py:278
  901.4 18.1 %collective-permute-start.52 = (bf16[4,1,2,48,1152]{4,3,2,1,0:T(8,128)(2,1)S(1)}, bf16[4,1,2,48,1152]{4,3,2,1,0:T(8,128)(2,1)S(1)}, u32[]{:S(2)}, u32[]{:S(2)}) collective-permute-start(bf16[4,1,2,48,1152]{4,3,2,1,0:T(8,128)(2,1)S(1)} %dynamic-slice_convert_fusion.3), channel_id=1, source_target_pairs={{0,4},{2,6},{4,0},{6,2},{8,12},{10,14},{12,8},{14,10},{16,20},{18,... | collective-permute-start | bytes 2654216 | tf_op jit(solution)/shard_map/ppermute | solution.py:278
  920.9 20.5 %collective-permute-start.83 = (f32[24,256]{1,0:T(8,128)S(1)}, f32[24,256]{1,0:T(8,128)S(1)}, u32[]{:S(2)}, u32[]{:S(2)}) collective-permute-start(f32[24,256]{1,0:T(8,128)S(1)} %get-tuple-element.214), channel_id=1, source_target_pairs={{0,1},{1,0},{2,3},{3,2},{4,5},{5,4},{6,7},{7,6},{8,9},{9,8},{10,11... | collective-permute-start | bytes 73736 | tf_op jit(solution)/shard_map/ppermute | solution.py:327
  921.0 24.3 %collective-permute-start.65 = (f32[24,1536]{1,0:T(8,128)S(1)}, f32[24,1536]{1,0:T(8,128)S(1)}, u32[]{:S(2)}, u32[]{:S(2)}) collective-permute-start(f32[24,1536]{1,0:T(8,128)S(1)} %get-tuple-element.193), channel_id=1, source_target_pairs={{0,1},{1,0},{2,3},{3,2},{4,5},{5,4},{6,7},{7,6},{8,9},{9,8},{10,11... | collective-permute-start | bytes 442376 | tf_op jit(solution)/shard_map/ppermute | solution.py:327
  (178 other events, 2526.2 us)
Sparse Core Ops, SparseCore 0:
  87.3 10.8 all-gather.9
  100.3 10.9 all-gather.7
  114.7 89.1 all-gather.5
  669.0 8.6 reduce-scatter.5
  713.5 9.1 reduce-scatter.3
  738.2 129.0 reduce-scatter.7

commit v2 on v0

v2 whole, which is shorter than its diff:
```python
import math

import jax
import jax.numpy as jnp
from jax import lax
from jax.experimental import pallas as pl
from jax.experimental.pallas import tpu as pltpu
from jax.sharding import PartitionSpec as P

HEADS = 12
HEAD_DIM = 64
DD = 512
DHEADS = 16
DHEAD_DIM = 32
PATCHES = 196
SEQ = 1024
IMG_SEQ = 16


EPSILON = 1e-06
NEGATIVE = -1e30


def position_table(model_width):
    grid_side = math.isqrt(PATCHES)
    patch_index = jnp.arange(PATCHES)
    row_coord = (patch_index // grid_side).astype(jnp.float32)[:, None]
    col_coord = (patch_index % grid_side).astype(jnp.float32)[:, None]
    quarter = model_width // 4
    frequency = jnp.power(10000.0, -jnp.arange(quarter).astype(jnp.float32) / quarter)[None, :]
    return jnp.concatenate(
        [
            jnp.sin(row_coord * frequency),
            jnp.cos(row_coord * frequency),
            jnp.sin(col_coord * frequency),
            jnp.cos(col_coord * frequency),
        ],
        axis=1,
    )


SWAP = [(0, 1), (1, 0)]
GATHER_ORDERS = ((0, 2, 1), (0, 1, 2), (2, 1, 0))


class Grid:
    def __init__(self, wide):
        dims, at = [1, 1, 1], 0
        while wide > 1:
            dims[at % 3] *= 2
            wide //= 2
            at += 1
        self.dims = tuple(dims)
        self.wide = dims[0] * dims[1] * dims[2]

    def split(self, wide_index):
        _, rows, cols = self.dims
        return (wide_index // (rows * cols), (wide_index // cols) % rows, wide_index % cols)

    def ring(self, axis):
        size = self.dims[axis]
        order = list(range(0, size, 2)) + list(range(size - 1, 0, -2))
        following = {order[k]: order[(k + 1) % size] for k in range(size)}
        pairs = []
        for source in range(self.wide):
            place = list(self.split(source))
            place[axis] = following[place[axis]]
            pairs.append((source, (place[0] * self.dims[1] + place[1]) * self.dims[2] + place[2]))
        return pairs

    def own(self, axis):
        return self.split(lax.axis_index("wide"))[axis]

    def behind(self, axis, steps):
        size, own = self.dims[axis], self.own(axis)
        if size == 2:
            return (own + steps) % 2
        place = jnp.where(own % 2 == 0, own // 2, size - 1 - own // 2)
        place = (place - steps + size) % size
        return jnp.where(place < size // 2, 2 * place, 2 * (size - place) - 1)


def gather_axis(grid, block, axis):
    size = grid.dims[axis]
    if size == 1:
        return block
    shape = list(block.shape)
    shape[axis] = size
    whole = jnp.zeros(tuple(shape), block.dtype)
    whole = lax.dynamic_update_slice_in_dim(whole, block, grid.own(axis), axis)
    for step in range(1, size):
        block = lax.ppermute(block, "wide", grid.ring(axis))
        whole = lax.dynamic_update_slice_in_dim(whole, block, grid.behind(axis, step), axis)
    return whole


def scatter_axis(grid, terms, axis):
    size = grid.dims[axis]

    def term(step):
        at = grid.behind(axis, step % size)
        slices = [lax.dynamic_slice_in_dim(t, at, 1, axis).astype(jnp.float32) for t in terms]
        return sum(slices[1:], slices[0])

    if size == 1:
        return sum([t.astype(jnp.float32) for t in terms[1:]], terms[0].astype(jnp.float32))
    total = term(1)
    for step in range(2, size + 1):
        got = lax.ppermute(total.astype(jnp.bfloat16), "wide", grid.ring(axis))
        total = got.astype(jnp.float32) + term(step)
    return total


def gather_parts(grid, parts):
    gathered = []
    for k, part in enumerate(parts):
        block = part[None, None, None]
        for axis in GATHER_ORDERS[k % 3]:
            block = gather_axis(grid, block, axis)
        gathered.append(block.reshape((grid.wide,) + part.shape))
    return gathered


def scatter_part(grid, terms, order):
    columns = terms[0].shape[-1]
    terms = [t.reshape(grid.dims + (-1, columns)) for t in terms]
    for axis in order:
        terms = [scatter_axis(grid, terms, axis)]
    return terms[0].reshape(-1, columns)


def regroup(array, block, start, width, groups=None):
    blocks, old = array.shape[:2]
    if old == block:
        return array
    groups = groups or (array.shape[2] - start) // width
    stop = start + groups * width
    rows = array[:, :, start:stop].reshape(blocks, old, groups, width).transpose(0, 2, 1, 3)
    rows = rows.reshape(-1, groups, block, width).transpose(0, 2, 1, 3).reshape(-1, block, groups * width)
    sides = [array[:, :, :start], array[:, :, stop:]]
    sides = [x.reshape(-1, block, x.shape[2]) if x.shape[2] else None for x in sides]
    return jnp.concatenate([x for x in (sides[0], rows, sides[1]) if x is not None], axis=2)


def halves(array, core):
    width = array.shape[-1] // 2
    own = lax.dynamic_slice_in_dim(array, core * width, width, array.ndim - 1)
    other = lax.dynamic_slice_in_dim(array, (1 - core) * width, width, array.ndim - 1)
    return own, other


def in_order(own, other, core, axis):
    return jnp.where(
        core == 0,
        jnp.concatenate([own, other], axis=axis),
        jnp.concatenate([other, own], axis=axis),
    )


def chip_rows(array, core):
    own, other = halves(array, core)
    return in_order(own, lax.ppermute(other, "narrow", SWAP), core, 0)


def core_rows(array, core):
    rows = array.shape[0] // 2
    own = lax.dynamic_slice_in_dim(array, core * rows, rows, 0)
    other = lax.dynamic_slice_in_dim(array, (1 - core) * rows, rows, 0)
    return in_order(own, lax.ppermute(other, "narrow", SWAP), core, 1)


ENC_BLOCK = 48
DEC_BLOCK = 16
LOG2E = 1.4426950408889634
PAD = 208
LIMIT = 56 * 2**20


def dot_nn(a, b):
    return jnp.dot(a, b, preferred_element_type=jnp.float32)


def dot_nt(a, b):
    return lax.dot_general(a, b, (((1,), (1,)), ((), ())), preferred_element_type=jnp.float32)


def dot_tn(a, b):
    return lax.dot_general(a, b, (((0,), (0,)), ((), ())), preferred_element_type=jnp.float32)


def low(values):
    return values.astype(jnp.bfloat16)


def norm_stats(values):
    center = values - jnp.mean(values, axis=-1, keepdims=True)
    scale = lax.rsqrt(jnp.mean(center * center, axis=-1, keepdims=True) + EPSILON)
    return center * scale, scale


def norm_apply(values, gain, bias):
    unit, _ = norm_stats(values)
    return unit * gain + bias


def norm_back(values, gain, d_normed):
    unit, scale = norm_stats(values)
    d_unit = d_normed * gain
    mean_d = jnp.mean(d_unit, axis=-1, keepdims=True)
    mean_du = jnp.mean(d_unit * unit, axis=-1, keepdims=True)
    d_values = scale * (d_unit - mean_d - unit * mean_du)
    return (
        d_values,
        jnp.sum(d_normed * unit, axis=0, keepdims=True),
        jnp.sum(d_normed, axis=0, keepdims=True),
    )


def gelu_parts(u):
    size = jnp.abs(u)
    t = 1.0 / (1.0 + (0.3275911 * 0.7071067811865476) * size)
    bell = jnp.exp2(u * u * (-0.5 * LOG2E))
    tail = t * (
        0.127414796 + t * (-0.142248368 + t * (0.7107068705 + t * (-0.7265760135 + t * 0.5307027145)))
    )
    tail = tail * bell
    phi = jnp.where(u >= 0, 1.0 - tail, tail)
    return phi, u * bell * 0.3989422804014327


def full_spec(shape):
    zeros = (0,) * len(shape)
    return pl.BlockSpec(shape, lambda *_: zeros)


def lead_spec(shape, count):
    zeros = (0,) * (len(shape) - 1)
    return pl.BlockSpec((count,) + tuple(shape[1:]), lambda i: (i,) + zeros)


def call(body, grid, ins, in_specs, outs, out_specs, scratch, flops, name, aliases=None):
    moved = sum(x.size * x.dtype.itemsize for x in list(ins) + list(outs))
    return pl.pallas_call(
        body,
        grid=grid,
        in_specs=in_specs,
        out_specs=out_specs,
        out_shape=outs,
        scratch_shapes=scratch,
        compiler_params=pltpu.CompilerParams(vmem_limit_bytes=LIMIT),
        cost_estimate=pl.CostEstimate(flops=flops, bytes_accessed=moved, transcendentals=0),
        input_output_aliases=aliases or {},
        name=name,
    )(*ins)


def begin(pairs, sems, first=0):
    copies = [
        pltpu.make_async_copy(source, target, sems.at[first + k])
        for k, (source, target) in enumerate(pairs)
    ]
    for copy in copies:
        copy.start()
    return copies


def finish(copies):
    for copy in copies:
        copy.wait()


def lanes_of(core, width):
    return pl.ds(pl.multiple_of(core * width, 128), width)


ANY = pl.BlockSpec(memory_space=pl.ANY)
SMEM = pl.BlockSpec(memory_space=pltpu.SMEM)


def f32(*shape):
    return jax.ShapeDtypeStruct(shape, jnp.float32)


def b16(*shape):
    return jax.ShapeDtypeStruct(shape, jnp.bfloat16)


def place_head(rows, slot, count):
    pieces = []
    if slot:
        pieces.append(jnp.zeros((slot * rows.shape[0], rows.shape[1]), rows.dtype))
    pieces.append(rows)
    if slot < count - 1:
        pieces.append(jnp.zeros(((count - 1 - slot) * rows.shape[0], rows.shape[1]), rows.dtype))
    return jnp.concatenate(pieces, axis=0)


def keep_lanes(values, slot, width):
    lane = lax.broadcasted_iota(jnp.int32, values.shape, 1)
    inside = (lane >= slot * width) & (lane < (slot + 1) * width)
    return jnp.where(inside, values, jnp.zeros_like(values))


def dec_attention_body(
    key_ref, e_ref, posn_ref, vec_ref, wqkv_ref, wo_ref,
    z_ref, qkv_ref, o_ref, m_ref, p_ref, il_ref, ot_ref,
    qt_s, vt_s, ot_s,
):
    step = pl.program_id(0)
    count, rows, width = z_ref.shape
    heads = p_ref.shape[1]
    head = width // heads
    group = 128 // head
    kappa = head ** (-0.5) * LOG2E
    for j in range(count):
        wanted = lax.broadcasted_iota(jnp.int32, (rows, 1), 0) + (step * count + j) * 256
        match = (key_ref[...] == wanted).astype(jnp.float32)
        seen = jnp.sum(match, axis=1, keepdims=True)
        z_ref[j] = dot_nn(low(match), e_ref[...]) + (1.0 - seen) * vec_ref[4:5] + posn_ref[...]
    z = z_ref[...].reshape(count * rows, width)
    n1 = low(norm_apply(z, vec_ref[0:1], vec_ref[1:2]))
    qkv_ref[...] = low(dot_nn(n1, wqkv_ref[...])).reshape(count, rows, 3 * width)

    def one_image(j, carry):
        qt_s[...] = qkv_ref[j, :, 0:width].T
        vt_s[...] = qkv_ref[j, :, 2 * width : 3 * width].T
        for h in range(heads):
            quad, slot = divmod(h, group)
            keys = qkv_ref[j, :, width + 128 * quad : width + 128 * (quad + 1)]
            s = dot_nn(keys, place_head(qt_s[h * head : (h + 1) * head], slot, group))
            tail = lax.broadcasted_iota(jnp.int32, (16, rows), 0) < PATCHES - (rows - 16)
            s = jnp.concatenate([s[: rows - 16], jnp.where(tail, s[rows - 16 :], NEGATIVE)], axis=0)
            p = jnp.exp2((s - jnp.max(s, axis=0, keepdims=True)) * kappa)
            inverse = 1.0 / jnp.sum(p, axis=0, keepdims=True)
            p = low(p)
            p_ref[j, h] = p
            il_ref[j, h : h + 1] = inverse
            ot_s[h * head : (h + 1) * head] = dot_nn(vt_s[h * head : (h + 1) * head], p) * inverse
        ot_ref[j] = low(ot_s[...])
        o_ref[j] = low(ot_s[...].T)
        return carry

    lax.fori_loop(0, count, one_image, 0)
    m_ref[...] = (z + dot_nn(o_ref[...].reshape(count * rows, width), wo_ref[...])).reshape(
        count, rows, width
    )


def dec_attention(key, embedded, posn, vec, packed, images):
    width = packed.shape[0]
    two = 2
    outs = [
        f32(images, PAD, width),
        b16(images, PAD, 3 * width),
        b16(images, PAD, width),
        f32(images, PAD, width),
        b16(images, DHEADS, PAD, PAD),
        f32(images, DHEADS, PAD),
        b16(images, width, PAD),
    ]
    ins = [key, embedded, posn, vec, packed, packed]
    return call(
        dec_attention_body,
        (images // two,),
        ins,
        [full_spec(x.shape) for x in ins[:4]]
        + [pl.BlockSpec((width, 3 * width), lambda i: (0, 0)), pl.BlockSpec((width, width), lambda i: (0, 3))],
        outs,
        [lead_spec(x.shape, two) for x in outs],
        [
            pltpu.VMEM((width, PAD), jnp.bfloat16),
            pltpu.VMEM((width, PAD), jnp.bfloat16),
            pltpu.VMEM((width, PAD), jnp.float32),
        ],
        2 * images * PAD * (4 * width * width + 2 * PAD * width * 4),
        "decoder_attention",
    )


def dec_mlp_body(
    m_ref, ct_ref, vec_ref, up_ref, packed_ref,
    out_ref, dm_ref, grads_ref, gvec_ref,
    ct_s, up_s, down_s, vec_s, w_s, low_s, sems,
):
    step, last = pl.program_id(0), pl.num_programs(0) - 1
    count, rows, width = m_ref.shape
    hidden = up_ref.shape[1]
    blocks, block = packed_ref.shape[:2]
    groups = hidden // (blocks * block)
    columns = [slice(4 * width + hidden + k * width, 4 * width + hidden + (k + 1) * width) for k in range(groups)]
    parts = [slice(k * block, (k + 1) * block) for k in range(groups)]

    @pl.when(step == 0)
    def _():
        up_s[...] = jnp.zeros_like(up_s)
        down_s[...] = jnp.zeros_like(down_s)
        vec_s[...] = jnp.zeros_like(vec_s)
        ct_s[...] = jnp.zeros_like(ct_s)
        finish(begin([(packed_ref.at[:, :, columns[k]], w_s.at[:, parts[k]]) for k in range(groups)], sems))

    for j in range(count):
        ct_s[j, 0:PATCHES] = ct_ref[j].astype(jnp.float32)
    ct = ct_s[...].reshape(count * rows, width)
    d_out = low(ct)
    m = m_ref[...].reshape(count * rows, width)
    n2 = low(norm_apply(m, vec_ref[2:3], vec_ref[3:4]))
    y = m
    d_n2 = jnp.zeros_like(m)
    chunk = 512
    for at in range(0, hidden, chunk):
        up = up_ref[:, at : at + chunk]
        span = groups * block
        down = w_s[at // span : (at + chunk) // span].reshape(chunk, width)
        u = dot_nn(n2, up)
        phi, slope = gelu_parts(u)
        g = low(u * phi)
        y = y + dot_nn(g, down)
        d_u = low(dot_nt(d_out, down) * (phi + slope))
        d_n2 = d_n2 + dot_nt(d_u, up)
        down_s[at : at + chunk] += dot_tn(g, d_out)
        up_s[:, at : at + chunk] += dot_tn(n2, d_u)
    for j in range(count):
        out_ref[j] = low(y[j * rows : j * rows + PATCHES])
    d_m, g_gain, g_bias = norm_back(m, vec_ref[2:3], d_n2)
    dm_ref[...] = (ct + d_m).reshape(count, rows, width)
    vec_s[0:1] += g_gain
    vec_s[1:2] += g_bias

    @pl.when(step == last)
    def _():
        gvec_ref[...] = vec_s[...]
        w_s[...] = low(down_s[...]).reshape(w_s.shape)
        low_s[...] = low(up_s[...]).reshape(low_s.shape)
        pairs = [(w_s.at[:, parts[k]], grads_ref.at[:, :, columns[k]]) for k in range(groups)]
        pairs.append((low_s, grads_ref.at[:, :, slice(4 * width, 4 * width + hidden)]))
        finish(begin(pairs, sems))


def dec_mlp(m, cotangent, vec, packed):
    images, rows, width = m.shape
    blocks, block, columns = packed.shape
    hidden = (columns - 4 * width) // 2
    two = 2
    ins = [m, cotangent, vec, packed.reshape(blocks * block, columns), packed]
    outs = [b16(images, PATCHES, width), f32(images, rows, width), b16(blocks, block, columns), f32(8, width)]
    return call(
        dec_mlp_body,
        (images // two,),
        ins,
        [
            lead_spec(m.shape, two),
            lead_spec(cotangent.shape, two),
            full_spec(vec.shape),
            pl.BlockSpec((width, hidden), lambda i: (0, 4 * width // hidden)),
            ANY,
        ],
        outs,
        [lead_spec(outs[0].shape, two), lead_spec(outs[1].shape, two), ANY, full_spec(outs[3].shape)],
        [
            pltpu.VMEM((two, rows, width), jnp.float32),
            pltpu.VMEM((width, hidden), jnp.float32),
            pltpu.VMEM((hidden, width), jnp.float32),
            pltpu.VMEM((8, width), jnp.float32),
            pltpu.VMEM((blocks, hidden // blocks, width), jnp.bfloat16),
            pltpu.VMEM((blocks, block, hidden), jnp.bfloat16),
            pltpu.SemaphoreType.DMA((8,)),
        ],
        12 * images * rows * width * hidden,
        "decoder_mlp",
    )


def dec_back_body(
    key_ref, keycol_ref, vec_ref, wqkv_ref, wo_ref,
    dm_ref, z_ref, qkv_ref, o_ref, p_ref, il_ref, ot_ref, given_ref,
    de_ref, gvec_ref, grads_ref,
    low_s, sem, de_s, gqkv_s, gwo_s, vec_s, dov_s, dot_s, dos_s, kt_s, dqt_s, dqkv_s,
):
    step, last = pl.program_id(0), pl.num_programs(0) - 1
    count, rows, width = z_ref.shape
    heads = p_ref.shape[1]
    head = width // heads
    group = 128 // head
    scale = head ** (-0.5)

    @pl.when(step == 0)
    def _():
        de_s[...] = jnp.zeros_like(de_s)
        gqkv_s[...] = jnp.zeros_like(gqkv_s)
        gwo_s[...] = jnp.zeros_like(gwo_s)
        vec_s[...] = jnp.zeros_like(vec_s)

    dm = dm_ref[...].reshape(count * rows, width)
    dmb = low(dm)
    gwo_s[...] += dot_tn(o_ref[...].reshape(count * rows, width), dmb)
    dov_s[...] = dot_nt(dmb, wo_ref[...]).reshape(count, rows, width)

    def one_image(j, carry):
        dot_s[...] = dov_s[j].T
        for h in range(heads):
            at = slice(h * head, (h + 1) * head)
            dot_s[at] = dot_s[at] * il_ref[j, h : h + 1]
        dos_s[...] = low(dot_s[...].T)
        kt_s[...] = qkv_ref[j, :, width : 2 * width].T
        for quad in range(width // 128):
            lanes = slice(quad * 128, (quad + 1) * 128)
            queries = qkv_ref[j, :, quad * 128 : (quad + 1) * 128]
            values = qkv_ref[j, :, 2 * width + quad * 128 : 2 * width + (quad + 1) * 128]
            d_rows = dos_s[:, lanes]
            d_k = jnp.zeros((rows, 128), jnp.float32)
            d_v = jnp.zeros((rows, 128), jnp.float32)
            for slot in range(group):
                h = quad * group + slot
                at = slice(h * head, (h + 1) * head)
                d_head = dot_s[at]
                delta = jnp.sum(ot_ref[j, at].astype(jnp.float32) * d_head, axis=0, keepdims=True)
                p = p_ref[j, h]
                d_p = dot_nn(values, place_head(low(d_head), slot, group))
                d_s = low(p.astype(jnp.float32) * (d_p - delta))
                d_v = d_v + dot_nn(p, keep_lanes(d_rows, slot, head))
                d_k = d_k + dot_nn(d_s, keep_lanes(queries, slot, head))
                dqt_s[at] = dot_nn(kt_s[at], d_s)
            dqkv_s[j, :, width + quad * 128 : width + (quad + 1) * 128] = low(d_k * scale)
            dqkv_s[j, :, 2 * width + quad * 128 : 2 * width + (quad + 1) * 128] = low(d_v)
        dqkv_s[j, :, 0:width] = low(dqt_s[...].T * scale)
        return carry

    lax.fori_loop(0, count, one_image, 0)
    d_qkv = dqkv_s[...].reshape(count * rows, 3 * width)
    z = z_ref[...].reshape(count * rows, width)
    n1 = low(norm_apply(z, vec_ref[0:1], vec_ref[1:2]))
    gqkv_s[...] += dot_tn(n1, d_qkv)
    d_z, g_gain, g_bias = norm_back(z, vec_ref[0:1], dot_nt(d_qkv, wqkv_ref[...]))
    d_z = dm + d_z
    vec_s[0:1] += g_gain
    vec_s[1:2] += g_bias
    for j in range(count):
        d_one = d_z[j * rows : (j + 1) * rows]
        base = (step * count + j) * 256
        wanted = lax.broadcasted_iota(jnp.int32, (rows, 1), 0) + base
        seen = jnp.sum((key_ref[...] == wanted).astype(jnp.float32), axis=1, keepdims=True)
        vec_s[2:3] += jnp.sum((1.0 - seen) * d_one, axis=0, keepdims=True)
        wanted = lax.broadcasted_iota(jnp.int32, (1, rows), 1) + base
        match = low((keycol_ref[...] == wanted).astype(jnp.float32))
        de_s[...] += dot_nn(match, low(d_one))

    @pl.when(step == last)
    def _():
        de_ref[...] = low(de_s[...])
        gvec_ref[...] = vec_s[...]
        blocks, block = low_s.shape[:2]
        low_s[:, :, 0 : 3 * width] = low(gqkv_s[...]).reshape(blocks, block, 3 * width)
        low_s[:, :, 3 * width :] = low(gwo_s[...]).reshape(blocks, block, width)
        copy = pltpu.make_async_copy(low_s, grads_ref.at[:, :, 0 : 4 * width], sem)
        copy.start()
        copy.wait()


def dec_back(key, keycol, vec, packed, dm, z, qkv, o, p, il, ot, grads):
    images, rows, width = z.shape
    two = 2
    seq = key.shape[1]
    ins = [key, keycol, vec, packed, packed, dm, z, qkv, o, p, il, ot, grads]
    outs = [b16(seq, width), f32(8, width), b16(*grads.shape)]
    return call(
        dec_back_body,
        (images // two,),
        ins,
        [full_spec(x.shape) for x in ins[:3]]
        + [pl.BlockSpec((width, 3 * width), lambda i: (0, 0)), pl.BlockSpec((width, width), lambda i: (0, 3))]
        + [lead_spec(x.shape, two) for x in ins[5:12]]
        + [ANY],
        outs,
        [full_spec(x.shape) for x in outs[:2]] + [ANY],
        [
            pltpu.VMEM(grads.shape[:2] + (4 * width,), jnp.bfloat16),
            pltpu.SemaphoreType.DMA(()),
            pltpu.VMEM((seq, width), jnp.float32),
            pltpu.VMEM((width, 3 * width), jnp.float32),
            pltpu.VMEM((width, width), jnp.float32),
            pltpu.VMEM((8, width), jnp.float32),
            pltpu.VMEM((two, rows, width), jnp.float32),
            pltpu.VMEM((width, rows), jnp.float32),
            pltpu.VMEM((rows, width), jnp.bfloat16),
            pltpu.VMEM((width, rows), jnp.bfloat16),
            pltpu.VMEM((width, rows), jnp.float32),
            pltpu.VMEM((two, rows, 3 * width), jnp.bfloat16),
        ],
        2 * images * rows * (8 * width * width + 5 * rows * width * 4),
        "decoder_attention_back",
        {12: 2},
    )


def enc_attention_body(
    core_ref, own_ref, win_ref, segq_ref, segk_ref, mine_ref, other_ref,
    q_ref, kv_ref, o_ref, m_ref, p_ref, il_ref, ot_ref, vec_ref,
    wqkv_ref, wo_ref, cols_s, qt_s, vt_s, ot_s, bias_s, sems,
):
    step = pl.program_id(0)
    rows, width = m_ref.shape
    heads, keys = p_ref.shape[1], p_ref.shape[2]
    head = width // heads
    group = 128 // head
    kappa = head ** (-0.5) * LOG2E

    @pl.when(step == 0)
    def _():
        core = core_ref[0]
        pairs = []
        for half, ref in ((core, mine_ref), (1 - core, other_ref)):
            pairs += [
                (ref.at[:, 0 : 3 * width // 2], wqkv_ref.at[:, lanes_of(half, 3 * width // 2)]),
                (ref.at[:, 3 * width // 2 : 2 * width], wo_ref.at[:, lanes_of(half, width // 2)]),
                (ref.at[:, 2 * width : 2 * width + 128], cols_s.at[half]),
            ]
        finish(begin(pairs, sems))
        vec_ref[...] = cols_s[0].astype(jnp.float32).T[0:8]
        normed = low(norm_apply(win_ref[...].astype(jnp.float32), vec_ref[0:1], vec_ref[1:2]))
        kv_ref[...] = low(dot_nn(normed, wqkv_ref[:, width:]))

    x = own_ref[...].astype(jnp.float32)
    normed = low(norm_apply(x, vec_ref[0:1], vec_ref[1:2]))
    q_ref[...] = low(dot_nn(normed, wqkv_ref[:, 0:width]))
    qt_s[...] = q_ref[...].T
    window = pl.ds(pl.multiple_of(step * 128, 128), keys)
    vt_s[...] = kv_ref[window, width:].T
    bias_s[...] = jnp.where(segk_ref[window, :] == segq_ref[...], 0.0, NEGATIVE)
    for h in range(heads):
        pair, slot = divmod(h, group)
        at = slice(h * head, (h + 1) * head)
        keys_pair = kv_ref[window, 128 * pair : 128 * (pair + 1)]
        s = dot_nn(keys_pair, place_head(qt_s[at], slot, group)) + bias_s[...]
        p = jnp.exp2((s - jnp.max(s, axis=0, keepdims=True)) * kappa)
        inverse = 1.0 / jnp.sum(p, axis=0, keepdims=True)
        p = low(p)
        p_ref[0, h] = p
        il_ref[0, h : h + 1] = inverse
        ot_s[at] = dot_nn(vt_s[at], p) * inverse
    ot_ref[0] = low(ot_s[...])
    o_ref[...] = low(ot_s[...].T)
    m_ref[...] = x + dot_nn(o_ref[...], wo_ref[...])


def enc_attention(core, own, window, seg_own, seg_window, mine, other):
    rows, width = own.shape
    total = window.shape[0]
    half = rows // 2
    keys = total - 128
    ins = [core, own, window, seg_own, seg_window, mine, other]
    in_specs = [
        SMEM,
        lead_spec(own.shape, half),
        full_spec(window.shape),
        pl.BlockSpec((1, half), lambda i: (0, i)),
        full_spec(seg_window.shape),
        ANY,
        ANY,
    ]
    outs = [
        b16(rows, width),
        b16(total, 2 * width),
        b16(rows, width),
        f32(rows, width),
        b16(2, HEADS, keys, half),
        f32(2, 16, half),
        b16(2, width, half),
        f32(8, width),
    ]
    out_specs = (
        [
            lead_spec(outs[0].shape, half),
            full_spec(outs[1].shape),
            lead_spec(outs[2].shape, half),
            lead_spec(outs[3].shape, half),
        ]
        + [lead_spec(x.shape, 1) for x in outs[4:7]]
        + [full_spec(outs[7].shape)]
    )
    return call(
        enc_attention_body,
        (2,),
        ins,
        in_specs,
        outs,
        out_specs,
        [
            pltpu.VMEM((width, 3 * width), jnp.bfloat16),
            pltpu.VMEM((width, width), jnp.bfloat16),
            pltpu.VMEM((2, width, 128), jnp.bfloat16),
            pltpu.VMEM((width, half), jnp.bfloat16),
            pltpu.VMEM((width, keys), jnp.bfloat16),
            pltpu.VMEM((width, half), jnp.float32),
            pltpu.VMEM((keys, half), jnp.float32),
            pltpu.SemaphoreType.DMA((6,)),
        ],
        2 * rows * (4 * width * width + 4 * keys * width),
        "encoder_attention",
    )


CHUNK = 768


def mlp_weights(core, mine_up, other_up, mine_down, other_down, up_s, down_s, embed_s):
    half_up = up_s.shape[2] // 2
    half_down = down_s.shape[2] // 2
    block = mine_down.shape[1]
    ups, embeds, downs = [], [], []
    for half, up, down in ((core, mine_up, mine_down), (1 - core, other_up, other_down)):
        ups.append((up.at[:, :, 0:half_up], up_s.at[:, :, lanes_of(half, half_up)]))
        for k, ref in enumerate((up, down)):
            lanes = pl.ds(pl.multiple_of(half * 256 + k * 128, 128), 128)
            embeds.append((ref.at[:, :, half_up : half_up + 128], embed_s.at[:, :, lanes]))
        for k in range(down_s.shape[1] // block):
            downs.append(
                (
                    down.at[:, :, k * half_down : (k + 1) * half_down],
                    down_s.at[:, k * block : (k + 1) * block, lanes_of(half, half_down)],
                )
            )
    return ups, embeds, downs


def enc_mlp_body(
    core_ref, m_ref, vec_ref, mu_ref, ou_ref, md_ref, od_ref,
    g_ref, slope_ref, h_ref, e_ref,
    up_s, down_s, embed_s, n2_s, y_s, sems,
):
    step, last = pl.program_id(0), pl.num_programs(0) - 1
    width = m_ref.shape[1]
    ups, embeds, downs = mlp_weights(core_ref[0], mu_ref, ou_ref, md_ref, od_ref, up_s, down_s, embed_s)

    @pl.when(step == 0)
    def _():
        up_copies = begin(ups, sems)
        rest = begin(downs + embeds, sems, len(ups))
        m = m_ref[...]
        n2_s[...] = low(norm_apply(m, vec_ref[2:3], vec_ref[3:4]))
        y_s[...] = m
        finish(up_copies + rest)

    up = up_s[:, :, pl.ds(pl.multiple_of(step * CHUNK, CHUNK), CHUNK)].reshape(width, CHUNK)
    span = CHUNK // down_s.shape[1]
    down = down_s[pl.ds(step * span, span)].reshape(CHUNK, width)
    u = dot_nn(n2_s[...], up)
    phi, slope = gelu_parts(u)
    g = low(u * phi)
    g_ref[...] = g
    slope_ref[...] = low(phi + slope)
    y_s[...] += dot_nn(g, down)

    @pl.when(step == last)
    def _():
        h = low(y_s[...])
        h_ref[...] = h
        e_ref[...] = low(dot_nn(h, embed_s[...].reshape(width, embed_s.shape[2])))


def mlp_scratch(blocks, block, width, hidden, embed):
    return [
        pltpu.VMEM((blocks, block, hidden), jnp.bfloat16),
        pltpu.VMEM((blocks, hidden // blocks, width), jnp.bfloat16),
        pltpu.VMEM((blocks, block, embed), jnp.bfloat16),
    ]


def enc_mlp(core, m, vec, mine_up, other_up, mine_down, other_down, hidden):
    rows, width = m.shape
    blocks, block = mine_up.shape[:2]
    embed = DD
    ins = [core, m, vec, mine_up, other_up, mine_down, other_down]
    outs = [b16(rows, hidden), b16(rows, hidden), b16(rows, width), b16(rows, embed)]
    columns = pl.BlockSpec((rows, CHUNK), lambda i: (0, i))
    return call(
        enc_mlp_body,
        (hidden // CHUNK,),
        ins,
        [SMEM, full_spec(m.shape), full_spec(vec.shape), ANY, ANY, ANY, ANY],
        outs,
        [columns, columns, full_spec(outs[2].shape), full_spec(outs[3].shape)],
        mlp_scratch(blocks, block, width, hidden, embed)
        + [
            pltpu.VMEM((rows, width), jnp.bfloat16),
            pltpu.VMEM((rows, width), jnp.float32),
            pltpu.SemaphoreType.DMA((16,)),
        ],
        4 * rows * width * hidden,
        "encoder_mlp",
    )


def enc_mlp_back_body(
    core_ref, de_ref, h_ref, m_ref, vec_ref, g_ref, slope_ref, mu_ref, ou_ref, md_ref, od_ref,
    umine_ref, uother_ref, dmine_ref, dother_ref, dm_ref, gvec_ref,
    up_s, down_s, embed_s, gup_s, gdown_s, n2t_s, dy_s, dyb_s, dn2_s, sems, out_sems,
):
    step, last = pl.program_id(0), pl.num_programs(0) - 1
    width = m_ref.shape[1]
    embed = embed_s.shape[2]
    core = core_ref[0]
    ups, embeds, downs = mlp_weights(core, mu_ref, ou_ref, md_ref, od_ref, up_s, down_s, embed_s)

    @pl.when(step == 0)
    def _():
        first = begin(embeds, sems)
        rest = begin(downs + ups, sems, len(embeds))
        n2t_s[...] = low(norm_apply(m_ref[...], vec_ref[2:3], vec_ref[3:4])).T
        dn2_s[...] = jnp.zeros_like(dn2_s)
        finish(first)
        d_y = dot_nt(de_ref[...], embed_s[...].reshape(width, embed))
        dy_s[...] = d_y
        dyb_s[...] = low(d_y)
        embed_s[...] = low(dot_tn(h_ref[...], de_ref[...])).reshape(embed_s.shape)
        finish(rest)

    columns = pl.ds(pl.multiple_of(step * CHUNK, CHUNK), CHUNK)
    span = CHUNK // down_s.shape[1]
    groups = pl.ds(step * span, span)
    up = up_s[:, :, columns].reshape(width, CHUNK)
    down = down_s[groups].reshape(CHUNK, width)
    d_out = dyb_s[...]
    d_u = low(dot_nt(d_out, down) * slope_ref[...].astype(jnp.float32))
    gdown_s[groups] = low(dot_tn(g_ref[...], d_out)).reshape(span, down_s.shape[1], width)
    gup_s[:, :, columns] = low(dot_nn(n2t_s[...], d_u)).reshape(up_s.shape[0], up_s.shape[1], CHUNK)
    dn2_s[...] += dot_nt(d_u, up)

    @pl.when(step == last)
    def _():
        sent = mlp_weights(core, umine_ref, uother_ref, dmine_ref, dother_ref, gup_s, gdown_s, embed_s)
        copies = begin([(target, source) for source, target in sent[0] + sent[1] + sent[2]], out_sems)
        d_m, g_gain, g_bias = norm_back(m_ref[...], vec_ref[2:3], dn2_s[...])
        dm_ref[...] = dy_s[...] + d_m
        gvec_ref[...] = jnp.concatenate(
            [g_gain, g_bias, jnp.zeros((6, g_gain.shape[1]), jnp.float32)], axis=0
        )
        finish(copies)


def enc_mlp_back(core, de, h, m, vec, g, slope, mine_up, other_up, mine_down, other_down):
    rows, width = m.shape
    hidden = g.shape[1]
    blocks, block, columns = mine_up.shape
    embed = de.shape[1]
    ins = [core, de, h, m, vec, g, slope, mine_up, other_up, mine_down, other_down]
    spec = pl.BlockSpec((rows, CHUNK), lambda i: (0, i))
    outs = [b16(blocks, block, columns)] * 4 + [f32(rows, width), f32(8, width)]
    scratch = mlp_scratch(blocks, block, width, hidden, embed)
    return call(
        enc_mlp_back_body,
        (hidden // CHUNK,),
        ins,
        [SMEM] + [full_spec(x.shape) for x in ins[1:5]] + [spec, spec, ANY, ANY, ANY, ANY],
        outs,
        [ANY] * 4 + [full_spec(x.shape) for x in outs[4:]],
        scratch
        + scratch[:2]
        + [
            pltpu.VMEM((width, rows), jnp.bfloat16),
            pltpu.VMEM((rows, width), jnp.float32),
            pltpu.VMEM((rows, width), jnp.bfloat16),
            pltpu.VMEM((rows, width), jnp.float32),
            pltpu.SemaphoreType.DMA((16,)),
            pltpu.SemaphoreType.DMA((16,)),
        ],
        8 * rows * width * hidden,
        "encoder_mlp_back",
    )


def enc_attention_back_body(
    core_ref, dm_ref, q_ref, kv_ref, p_ref, il_ref, ot_ref, mine_ref, other_ref,
    dq_ref, dkv_ref,
    wo_ref, dot_s, dos_s, kt_s, dqt_s, sems,
):
    step = pl.program_id(0)
    rows, width = dm_ref.shape
    heads, keys = p_ref.shape[1], p_ref.shape[2]
    head = width // heads
    group = 128 // head
    scale = head ** (-0.5)

    @pl.when(step == 0)
    def _():
        pairs = [
            (ref.at[:, 3 * width // 2 : 2 * width], wo_ref.at[:, lanes_of(half, width // 2)])
            for half, ref in ((core_ref[0], mine_ref), (1 - core_ref[0], other_ref))
        ]
        copies = begin(pairs, sems)
        dkv_ref[...] = jnp.zeros_like(dkv_ref)
        finish(copies)

    dmb = low(dm_ref[...])
    dot_s[...] = dot_nt(dmb, wo_ref[...]).T
    for h in range(heads):
        at = slice(h * head, (h + 1) * head)
        dot_s[at] = dot_s[at] * il_ref[0, h : h + 1]
    dos_s[...] = low(dot_s[...].T)
    window = pl.ds(pl.multiple_of(step * 128, 128), keys)
    kt_s[...] = kv_ref[window, 0:width].T
    for pair in range(width // 128):
        lanes = slice(pair * 128, (pair + 1) * 128)
        queries = q_ref[:, lanes]
        values = kv_ref[window, width + pair * 128 : width + (pair + 1) * 128]
        d_rows = dos_s[:, lanes]
        d_k = jnp.zeros((keys, 128), jnp.float32)
        d_v = jnp.zeros((keys, 128), jnp.float32)
        for slot in range(group):
            h = pair * group + slot
            at = slice(h * head, (h + 1) * head)
            d_head = dot_s[at]
            delta = jnp.sum(ot_ref[0, at].astype(jnp.float32) * d_head, axis=0, keepdims=True)
            p = p_ref[0, h]
            d_p = dot_nn(values, place_head(low(d_head), slot, group))
            d_s = low(p.astype(jnp.float32) * (d_p - delta))
            d_v = d_v + dot_nn(p, keep_lanes(d_rows, slot, head))
            d_k = d_k + dot_nn(d_s, keep_lanes(queries, slot, head))
            dqt_s[at] = dot_nn(kt_s[at], d_s)
        dkv_ref[window, pair * 128 : (pair + 1) * 128] += d_k * scale
        dkv_ref[window, width + pair * 128 : width + (pair + 1) * 128] += d_v
    dq_ref[...] = low(dqt_s[...].T * scale)


def enc_attention_back(core, dm, q, kv, p, il, ot, mine, other):
    rows, width = dm.shape
    total = kv.shape[0]
    half = rows // 2
    keys = total - 128
    ins = [core, dm, q, kv, p, il, ot, mine, other]
    block = lead_spec(dm.shape, half)
    outs = [b16(rows, width), f32(total, 2 * width)]
    return call(
        enc_attention_back_body,
        (2,),
        ins,
        [SMEM, block, block, full_spec(kv.shape)] + [lead_spec(x.shape, 1) for x in ins[4:7]] + [ANY, ANY],
        outs,
        [block, full_spec(outs[1].shape)],
        [
            pltpu.VMEM((width, width), jnp.bfloat16),
            pltpu.VMEM((width, half), jnp.float32),
            pltpu.VMEM((half, width), jnp.bfloat16),
            pltpu.VMEM((width, keys), jnp.bfloat16),
            pltpu.VMEM((width, half), jnp.float32),
            pltpu.SemaphoreType.DMA((2,)),
        ],
        2 * rows * (width * width + 10 * keys * width),
        "encoder_attention_back",
    )


def enc_qkv_back_body(
    core_ref, own_ref, dm_ref, o_ref, dq_ref, dkv_ref, got_ref, vec_ref, gvec2_ref, dvec_ref,
    mine_ref, other_ref,
    gmine_ref, gother_ref, dr_ref,
    wqkv_s, gqkv_s, gwo_s, cols_s, dqkv_s, sems, out_sems,
):
    rows, width = dm_ref.shape
    near = got_ref.shape[0]
    core = core_ref[0]
    halves_at = ((core, mine_ref, gmine_ref), (1 - core, other_ref, gother_ref))
    weights = begin(
        [
            (ref.at[:, 0 : 3 * width // 2], wqkv_s.at[:, lanes_of(half, 3 * width // 2)])
            for half, ref, _ in halves_at
        ],
        sems,
    )
    x = own_ref[...].astype(jnp.float32)
    n1t = low(norm_apply(x, vec_ref[0:1], vec_ref[1:2])).T
    gwo_s[...] = low(dot_tn(o_ref[...], low(dm_ref[...])))
    sent = begin(
        [
            (gwo_s.at[:, lanes_of(half, width // 2)], ref.at[:, 3 * width // 2 : 2 * width])
            for half, _, ref in halves_at
        ],
        out_sems,
    )
    dqkv_s[0] = dq_ref[...]
    first = pl.ds(pl.multiple_of(core * near, near), rows)
    edge = pl.ds(pl.multiple_of((1 - core) * (rows - near), near), near)
    edge_in = pl.ds(pl.multiple_of(core * near + (1 - core) * (rows - near), near), near)
    for k in range(2):
        lanes = slice(k * width, (k + 1) * width)
        dqkv_s[k + 1] = low(dkv_ref[first, lanes])
        dqkv_s[k + 1, edge] = low(dkv_ref[edge_in, lanes] + got_ref[:, lanes].astype(jnp.float32))
    finish(weights)
    d_n1 = jnp.zeros((rows, width), jnp.float32)
    for k in range(3):
        lanes = slice(k * width, (k + 1) * width)
        d_part = dqkv_s[k]
        gqkv_s[:, lanes] = low(dot_nn(n1t, d_part))
        d_n1 = d_n1 + dot_nt(d_part, wqkv_s[:, lanes])
    sent += begin(
        [
            (gqkv_s.at[:, lanes_of(half, 3 * width // 2)], ref.at[:, 0 : 3 * width // 2])
            for half, _, ref in halves_at
        ],
        out_sems,
        2,
    )
    d_r, g_gain, g_bias = norm_back(x, vec_ref[0:1], d_n1)
    dr_ref[...] = dm_ref[...] + d_r
    grads = jnp.concatenate(
        [g_gain, g_bias, gvec2_ref[0:2], jnp.zeros((124, width), jnp.float32)], axis=0
    )
    cols_s[0] = low(grads.T)
    cols_s[1] = dvec_ref[...]
    sent += begin(
        [(cols_s.at[half], ref.at[:, 2 * width : 2 * width + 128]) for half, _, ref in halves_at],
        out_sems,
        4,
    )
    finish(sent)


def enc_qkv_back(core, own, dm, o, dq, dkv, got, vec, gvec2, dvec, mine, other):
    rows, width = dm.shape
    ins = [core, own, dm, o, dq, dkv, got, vec, gvec2, dvec, mine, other]
    outs = [b16(*mine.shape), b16(*mine.shape), f32(rows, width)]
    return call(
        enc_qkv_back_body,
        (1,),
        ins,
        [SMEM] + [full_spec(x.shape) for x in ins[1:10]] + [ANY, ANY],
        outs,
        [ANY, ANY, full_spec(outs[2].shape)],
        [
            pltpu.VMEM((width, 3 * width), jnp.bfloat16),
            pltpu.VMEM((width, 3 * width), jnp.bfloat16),
            pltpu.VMEM((width, width), jnp.bfloat16),
            pltpu.VMEM((2, width, 128), jnp.bfloat16),
            pltpu.VMEM((3, rows, width), jnp.bfloat16),
            pltpu.SemaphoreType.DMA((2,)),
            pltpu.SemaphoreType.DMA((6,)),
        ],
        14 * rows * width * width,
        "encoder_qkv_back",
    )


def shards(
    inputs,
    enc_norm_gain,
    enc_norm_bias,
    enc_qkv,
    enc_proj,
    enc_mlp_gain,
    enc_mlp_bias,
    enc_up,
    enc_down,
    embed_weight,
    mask_token,
    dec_norm_gain,
    dec_norm_bias,
    dec_qkv,
    dec_proj,
    dec_mlp_gain,
    dec_mlp_bias,
    dec_up,
    dec_down,
    cotangent,
    visible_counts,
    patch_positions,
    image_owner,
):
    core = lax.axis_index("narrow").astype(jnp.int32)
    wide_index = lax.axis_index("wide")
    cores = lax.axis_size("narrow")
    grid = Grid(lax.axis_size("wide"))
    devices = grid.wide * cores
    half_rows = inputs.shape[1]
    slot_count = IMG_SEQ // cores
    rows_e, rows_d = enc_qkv.shape[0], dec_qkv.shape[0]
    width_e, width_d = enc_proj.shape[1], dec_proj.shape[1]
    wide_e, wide_d = enc_up.shape[1], dec_up.shape[1]
    half_q, half_p, half_u, half_v = 3 * width_e // 2, width_e // 2, wide_e // 2, width_d // 2

    vectors_e = jnp.stack([enc_norm_gain, enc_norm_bias, enc_mlp_gain, enc_mlp_bias], axis=1)
    vectors_d = jnp.stack(
        [dec_norm_gain, dec_norm_bias, dec_mlp_gain, dec_mlp_bias, mask_token], axis=1
    )
    packs = []
    for half, vectors in enumerate((vectors_e, vectors_d)):
        vectors = jnp.pad(vectors, ((0, rows_e - vectors.shape[0]), (0, 128 - vectors.shape[1])))
        packs.append(
            jnp.concatenate(
                [
                    enc_qkv[:, half * half_q : (half + 1) * half_q],
                    enc_proj[:, half * half_p : (half + 1) * half_p],
                    vectors,
                    enc_up[:, half * half_u : (half + 1) * half_u],
                    embed_weight[:, half * half_v : (half + 1) * half_v],
                ],
                axis=1,
            )
        )
    own_pack = jnp.where(core == 0, packs[0], packs[1])
    other_pack = jnp.where(core == 0, packs[1], packs[0])
    chip_pack = in_order(own_pack, lax.ppermute(other_pack, "narrow", SWAP), core, 0)
    chip_down = chip_rows(enc_down, core)
    chip_block = cores * rows_e
    down_groups = chip_down.shape[0] // chip_block
    part = half_q + half_p + 128
    parts = [
        chip_pack[:, :part],
        chip_pack[:, part : 2 * part],
        jnp.concatenate(
            [chip_down[k * chip_block : (k + 1) * chip_block] for k in range(down_groups)]
            + [chip_pack[:, 2 * part :]],
            axis=1,
        ),
    ]
    group_d = dec_down.shape[0] // rows_d
    dec_packed = jnp.concatenate(
        [dec_qkv, dec_proj, dec_up] + [dec_down[k * rows_d : (k + 1) * rows_d] for k in range(group_d)],
        axis=1,
    )
    dec_whole = lax.all_gather(dec_packed, ("wide", "narrow"), axis=0, tiled=True)
    dec_whole = regroup(
        dec_whole.reshape(devices, rows_d, dec_whole.shape[1]), DEC_BLOCK, 4 * width_d + wide_d, width_d
    )

    def full_parts(gathered):
        shaped = [gathered[k].reshape(-1, ENC_BLOCK, part) for k in range(2)]
        return shaped + [regroup(gathered[2], ENC_BLOCK, 0, half_p, down_groups)]

    wide_parts = gather_parts(grid, parts)
    mine = full_parts(wide_parts)
    other = full_parts([lax.ppermute(w, "narrow", SWAP) for w in wide_parts])
    mine_first, other_first = [x.reshape(width_e, part) for x in (mine[0], other[0])]
    vectors_two = jnp.where(core == 0, other_first[:, -128:], mine_first[:, -128:])
    vectors_two = vectors_two.reshape(devices, rows_e, 128)[:, :rows_d].reshape(width_d, 128)
    dec_rows = vectors_two.astype(jnp.float32).T[:8]

    image_ends = jnp.cumsum(visible_counts[0], axis=0)
    position = jnp.arange(SEQ, dtype=jnp.int32)
    segment_all = jnp.sum((image_ends[None, :] <= position[:, None]).astype(jnp.int32), axis=1)
    segment_own = lax.dynamic_slice_in_dim(segment_all, core * half_rows, half_rows, 0)
    other_positions = lax.ppermute(patch_positions[0], "narrow", SWAP)
    sequence_positions = in_order(patch_positions[0], other_positions, core, 0)
    owners = lax.dynamic_slice_in_dim(image_owner, wide_index * IMG_SEQ, IMG_SEQ, 0)
    local_slot = owners - (wide_index * cores + core) * slot_count
    slot_base = jnp.where((local_slot >= 0) & (local_slot < slot_count), local_slot * 256, -256)
    row_base = jnp.sum(
        jnp.where(segment_all[:, None] == jnp.arange(IMG_SEQ)[None, :], slot_base[None, :], 0), axis=1
    )
    key = jnp.where(row_base >= 0, row_base + sequence_positions, -1).astype(jnp.int32)
    posn = jnp.pad(position_table(width_d), ((0, PAD - PATCHES), (0, 0)))

    near = 128
    own_rows = inputs[0]
    edge = lax.dynamic_slice_in_dim(own_rows, (1 - core) * (half_rows - near), near, 0)
    window_rows = in_order(own_rows, lax.ppermute(edge, "narrow", SWAP), core, 0)
    seg_window = lax.dynamic_slice_in_dim(segment_all, core * (half_rows - near), half_rows + near, 0)
    core_one = core[None]
    queries, keys_values, context, middle, probs, inverse, context_t, enc_rows = enc_attention(
        core_one, own_rows, window_rows, segment_own[None, :], seg_window[:, None], mine_first, other_first
    )
    hidden_act, hidden_slope, encoded_low, embedded = enc_mlp(
        core_one, middle, enc_rows, mine[1], other[1], mine[2], other[2], wide_e
    )

    sequence_embedded = in_order(embedded, lax.ppermute(embedded, "narrow", SWAP), core, 0)
    dec_flat = dec_whole.reshape(width_d, dec_whole.shape[2])
    z, packed_d, context_d, middle_d, probs_d, inverse_d, context_td = dec_attention(
        key[None, :], sequence_embedded, posn, dec_rows, dec_flat, slot_count
    )
    decoded, d_middle_d, grads_d, grad_dec_vec2 = dec_mlp(middle_d, cotangent, dec_rows, dec_whole)
    d_sequence, grad_dec_vec1, grads_d = dec_back(
        key[None, :], key[:, None], dec_rows, dec_flat,
        d_middle_d, z, packed_d, context_d, probs_d, inverse_d, context_td, grads_d,
    )
    grads_d = regroup(grads_d, rows_d, 4 * width_d + wide_d, width_d)
    sum_d = lax.psum_scatter(
        grads_d.reshape(width_d, -1), ("wide", "narrow"), scatter_dimension=0, tiled=True
    )

    d_mine = lax.dynamic_slice_in_dim(d_sequence, core * half_rows, half_rows, 0)
    d_theirs = lax.dynamic_slice_in_dim(d_sequence, (1 - core) * half_rows, half_rows, 0)
    d_embedded = low(
        d_mine.astype(jnp.float32) + lax.ppermute(d_theirs, "narrow", SWAP).astype(jnp.float32)
    )
    up_mine, up_other, down_mine, down_other, d_middle, grad_vec2 = enc_mlp_back(
        core_one, d_embedded, encoded_low, middle, enc_rows, hidden_act, hidden_slope,
        mine[1], other[1], mine[2], other[2],
    )

    def summed(own, theirs, order):
        got = lax.ppermute(theirs, "narrow", SWAP)
        return scatter_part(grid, [own, got], order)

    sum_up = summed(up_mine, up_other, (2, 1, 0))
    sum_down = summed(
        *[regroup(x, chip_block, 0, half_p, down_groups) for x in (down_mine, down_other)], (1, 2, 0)
    )
    d_queries, d_keys_values = enc_attention_back(
        core_one, d_middle, queries, keys_values, probs, inverse, context_t, mine_first, other_first
    )
    d_far = lax.dynamic_slice_in_dim(d_keys_values, (1 - core) * half_rows, near, 0)
    d_got = lax.ppermute(low(d_far), "narrow", SWAP)
    columns_d = jnp.stack(
        [grad_dec_vec1[0], grad_dec_vec1[1], grad_dec_vec2[0], grad_dec_vec2[1], grad_dec_vec1[2]], axis=1
    )
    columns_d = jnp.pad(
        low(columns_d).reshape(devices, rows_d, 5), ((0, 0), (0, rows_e - rows_d), (0, 123))
    ).reshape(width_e, 128)
    first_mine, first_other, d_inputs = enc_qkv_back(
        core_one, own_rows, d_middle, context, d_queries, d_keys_values, d_got,
        enc_rows, grad_vec2, columns_d, mine_first, other_first,
    )
    cut = 896
    sum_first = jnp.concatenate(
        [
            summed(first_mine[:, :cut], first_other[:, :cut], (2, 1, 0)),
            summed(first_mine[:, cut:], first_other[:, cut:], (1, 2, 0)),
        ],
        axis=1,
    )

    groups = [sum_down[:, k * half_p : (k + 1) * half_p] for k in range(down_groups)]
    row_pack = jnp.concatenate([sum_first, sum_up, sum_down[:, down_groups * half_p :]], axis=1)
    out_down = core_rows(jnp.concatenate(groups, axis=0), core)
    own_out = lax.dynamic_slice_in_dim(row_pack, core * rows_e, rows_e, 0)
    send_out = lax.dynamic_slice_in_dim(row_pack, (1 - core) * rows_e, rows_e, 0)
    got_out = lax.ppermute(send_out, "narrow", SWAP)
    halves_out = [jnp.where(core == 0, own_out, got_out), jnp.where(core == 0, got_out, own_out)]

    def columns(start, count):
        return jnp.concatenate([x[:, start : start + count] for x in halves_out], axis=1)

    vec_e = halves_out[0][:, half_q + half_p : part]
    vec_d = halves_out[1][:rows_d, half_q + half_p : part]
    sum_d = sum_d.astype(jnp.float32)
    at_d = 4 * width_d + wide_d
    return (
        decoded,
        d_inputs.reshape(inputs.shape),
        vec_e[:, 0],
        vec_e[:, 1],
        columns(0, half_q),
        columns(half_q, half_p),
        vec_e[:, 2],
        vec_e[:, 3],
        columns(part, half_u),
        out_down,
        columns(part + half_u, half_v),
        vec_d[:, 4],
        vec_d[:, 0],
        vec_d[:, 1],
        sum_d[:, : 3 * width_d],
        sum_d[:, 3 * width_d : 4 * width_d],
        vec_d[:, 2],
        vec_d[:, 3],
        sum_d[:, 4 * width_d : at_d],
        jnp.concatenate(
            [sum_d[:, at_d + k * width_d : at_d + (k + 1) * width_d] for k in range(group_d)], axis=0
        ),
    )


def solution(mesh):
    in_specs = (
        P("wide", "narrow", None),
        P(("wide", "narrow")),
        P(("wide", "narrow")),
        P(("wide", "narrow"), None),
        P(("wide", "narrow"), None),
        P(("wide", "narrow")),
        P(("wide", "narrow")),
        P(("wide", "narrow"), None),
        P(("wide", "narrow"), None),
        P(("wide", "narrow"), None),
        P(("wide", "narrow")),
        P(("wide", "narrow")),
        P(("wide", "narrow")),
        P(("wide", "narrow"), None),
        P(("wide", "narrow"), None),
        P(("wide", "narrow")),
        P(("wide", "narrow")),
        P(("wide", "narrow"), None),
        P(("wide", "narrow"), None),
        P(("wide", "narrow"), None, None),
        P("wide", None),
        P("wide", "narrow"),
        P(),
    )
    out_specs = (
        P(("wide", "narrow"), None, None),
        P("wide", "narrow", None),
        P(("wide", "narrow")),
        P(("wide", "narrow")),
        P(("wide", "narrow"), None),
        P(("wide", "narrow"), None),
        P(("wide", "narrow")),
        P(("wide", "narrow")),
        P(("wide", "narrow"), None),
        P(("wide", "narrow"), None),
        P(("wide", "narrow"), None),
        P(("wide", "narrow")),
        P(("wide", "narrow")),
        P(("wide", "narrow")),
        P(("wide", "narrow"), None),
        P(("wide", "narrow"), None),
        P(("wide", "narrow")),
        P(("wide", "narrow")),
        P(("wide", "narrow"), None),
        P(("wide", "narrow"), None),
    )
    return jax.shard_map(shards, mesh=mesh, in_specs=in_specs, out_specs=out_specs, check_vma=False)
```

time: 1870 us -> 551 us (0.29)
  waiting for transfers between devices: 1060 us -> 174 us
  matrix products: 347 us -> 0 us
  Pallas kernels: 0 us -> 225 us
  blocking collectives: 176 us -> 0 us
  local copies, waits for them, and re-layouts: 144 us -> 49.3 us
  other arithmetic: 105 us -> 32.4 us
  starting transfers between devices: 4.6 us -> 48 us
    reduce_scatter x11 -> x1, waiting for transfers between devices: 999 us -> 19.1 us  [shards(): lax.psum_scatter(grads_d.reshape(width_d, -1), ('wide', 'narrow'), scatte...]
    dot_general x38 -> x0, matrix products: 331 us -> none  [the longest x9 86.3 us: product(): return jnp.dot(left_side, right_side, preferred_element_type=jnp.float32)]
    pallas_call x0 -> x8, Pallas kernels: none -> 225 us  [call(): pl.pallas_call(body, grid=grid, in_specs=in_specs, out_specs=out_specs, o...]
    ppermute x0 -> x51, waiting for transfers between devices: none -> 155 us  [the longest x20 79 us: scatter_axis(): got = lax.ppermute(total.astype(jnp.bfloat16), 'wide', grid.ring(axis))]
    all_gather x2 -> x0, blocking collectives: 83.2 us -> none  [the longest x1 43.5 us: shards(): lax.all_gather(dec_proj, ('wide', 'narrow'), axis=0, tiled=True)]
    unnamed x2 -> x0, blocking collectives: 81.7 us -> none
    all_gather x9 -> x1, waiting for transfers between devices: 58.2 us -> 0.01 us  [shards(): lax.all_gather(dec_packed, ('wide', 'narrow'), axis=0, tiled=True)]
    ppermute x0 -> x51, starting transfers between devices: none -> 47.9 us  [the longest x20 28 us: scatter_axis(): got = lax.ppermute(total.astype(jnp.bfloat16), 'wide', grid.ring(axis))]
  transfers between devices with their start and end apart: 21 -> 53, of which waited for: 13 -> 28; matrix products, arithmetic and copies ran while one was open for 21% -> 11% of each run, Pallas kernels for 0% -> 7%
where the time goes in v2:
time: 551 us; the launch traced here: 544 us
  Pallas kernels  225 us (41%)
  waiting for transfers between devices  174 us (32%)
  local copies, waits for them, and re-layouts  49.3 us (9%)
  starting transfers between devices  48 us (9%)
  other arithmetic  32.4 us (6%)
  between operations  15.6 us (3%)
    pallas_call x8, Pallas kernels, call(): pl.pallas_call(body, grid=grid, in_specs=in_specs, out_specs=out_specs, o...  225 us
    ppermute x20, waiting for transfers between devices, scatter_axis(): got = lax.ppermute(total.astype(jnp.bfloat16), 'wide', grid.ring(axis))  79 us
    ppermute x15, waiting for transfers between devices, gather_axis(): block = lax.ppermute(block, 'wide', grid.ring(axis))  75 us
    ppermute x20, starting transfers between devices, scatter_axis(): got = lax.ppermute(total.astype(jnp.bfloat16), 'wide', grid.ring(axis))  28 us
    reduce_scatter x1, waiting for transfers between devices, shards(): lax.psum_scatter(grads_d.reshape(width_d, -1), ('wide', 'narrow'), scatte...  19.1 us
    ppermute x15, starting transfers between devices, gather_axis(): block = lax.ppermute(block, 'wide', grid.ring(axis))  16.1 us
    unnamed x55, local copies, waits for them, and re-layouts  14.4 us
  transfers between devices with their start and end apart: 53, of which 28 were waited for; matrix products, arithmetic and copies ran while one was open for 11% of the time, Pallas kernels for 7%

profile of v2, /device:TPU:0, one launch (start us, length us, event | category | flops | bytes accessed | tf_op | source)
XLA Modules:
  0.0 544.1 jit_solution(1533586313390270797)
XLA Ops:
  17.4 4.1 collective-permute-start.3
  24.8 3.8 collective-permute-done.16
  32.0 7.0 %collective-permute-done.4 = bf16[1,1,1,48,1664]{4,3,2,1,0:T(8,128)(2,1)S(1)} collective-permute-done((bf16[1,1,1,48,1664]{4,3,2,1,0:T(8,128)(2,1)S(1)}, bf16[1,1,1,48,1664]{4,3,2,1,0:T(8,128)(2,1)S(1)}, u32[]{:S(2)}, u32[]{:S(2)}) %collective-permute-start.4) | collective-permute-done | bytes 159776 | tf_op jit(solution)/shard_map/ppermute | solution.py:92
  39.3 4.3 collective-permute-done.10
  45.0 2.3 collective-permute-done.5
  52.4 7.6 %collective-permute-done.6 = bf16[4,1,1,48,1664]{4,3,2,1,0:T(8,128)(2,1)S(1)} collective-permute-done((bf16[4,1,1,48,1664]{4,3,2,1,0:T(8,128)(2,1)S(1)}, bf16[4,1,1,48,1664]{4,3,2,1,0:T(8,128)(2,1)S(1)}, u32[]{:S(2)}, u32[]{:S(2)}) %collective-permute-start.6) | collective-permute-done | bytes 639008 | tf_op jit(solution)/shard_map/ppermute | solution.py:92
  60.8 8.0 %collective-permute-done.12 = bf16[4,1,1,48,1664]{4,3,2,1,0:T(8,128)(2,1)S(1)} collective-permute-done((bf16[4,1,1,48,1664]{4,3,2,1,0:T(8,128)(2,1)S(1)}, bf16[4,1,1,48,1664]{4,3,2,1,0:T(8,128)(2,1)S(1)}, u32[]{:S(2)}, u32[]{:S(2)}) %collective-permute-start.12) | collective-permute-done | bytes 639008 | tf_op jit(solution)/shard_map/ppermute | solution.py:92
  74.2 18.9 %collective-permute-done.19 = bf16[1,2,2,48,1664]{4,3,2,1,0:T(8,128)(2,1)S(1)} collective-permute-done((bf16[1,2,2,48,1664]{4,3,2,1,0:T(8,128)(2,1)S(1)}, bf16[1,2,2,48,1664]{4,3,2,1,0:T(8,128)(2,1)S(1)}, u32[]{:S(2)}, u32[]{:S(2)}) %collective-permute-start.19) | collective-permute-done | bytes 639008 | tf_op jit(solution)/shard_map/ppermute | solution.py:92
  96.2 22.5 %collective-permute-done.20 = bf16[1,2,2,48,1664]{4,3,2,1,0:T(8,128)(2,1)S(1)} collective-permute-done((bf16[1,2,2,48,1664]{4,3,2,1,0:T(8,128)(2,1)S(1)}, bf16[1,2,2,48,1664]{4,3,2,1,0:T(8,128)(2,1)S(1)}, u32[]{:S(2)}, u32[]{:S(2)}) %collective-permute-start.20) | collective-permute-done | bytes 639008 | tf_op jit(solution)/shard_map/ppermute | solution.py:92
  124.9 3.1 copy.86.ct_ref
  133.5 20.8 %encoder_attention.1 = (bf16[512,768]{1,0:T(8,128)(2,1)}, bf16[640,1536]{1,0:T(8,128)(2,1)}, bf16[512,768]{1,0:T(8,128)(2,1)}, f32[512,768]{1,0:T(8,128)}, bf16[...) custom-call(s32[1]{0:T(128)} %bitcast.4.core_ref, ...), custom_call_target="tpu_custom_call" | custom-call | flops 4026531840 | bytes 19132932 | tf_op jit(solution)/shard_map/encoder_attention/pallas_call | solution.py:243
  154.3 17.7 %encoder_mlp.1 = (bf16[512,3072]{1,0:T(8,128)(2,1)}, bf16[512,3072]{1,0:T(8,128)(2,1)}, bf16[512,768]{1,0:T(8,128)(2,1)}, bf16[512,512]{1,0:T(8,128)(2,1)}) custom-call(s32[1]{0:T(128)} %bitcast.4.core_ref, f32[512,768]{1,0:T(8,128)} %get-tuple-element.57.m_ref, f32[8,768]{1,0:T(8,128)} %get-tuple-element.58.vec_ref, bf16[16,48,1664]{2,1,0:T(8,128)(2,1)} %bitcast.22.mu_ref, ...), custom_call_target="tpu_custom_call" | custom-call | flops 4831838208 | bytes 19423236 | tf_op jit(solution)/shard_map/encoder_mlp/pallas_call | solution.py:243
  174.9 2.5 maximum_select_fusion.e_ref
  177.5 45.0 %decoder_attention.1 = (f32[8,208,512]{2,1,0:T(8,128)}, bf16[8,208,1536]{2,1,0:T(8,128)(2,1)}, bf16[8,208,512]{2,1,0:T(8,128)(2,1)}, f32[8,208,512]{2,1,0:T(8,12...) custom-call(s32[1,1024]{1,0:T(1,128)} %compare_select_fusion.key_ref, ...), custom_call_target="tpu_custom_call" | custom-call | flops 6325010432 | bytes 40595456 | tf_op jit(solution)/shard_map/decoder_attention/pallas_call | solution.py:243
  222.5 41.0 %decoder_mlp.1 = (bf16[8,196,512]{2,1,0:T(8,128)(2,1)}, f32[8,208,512]{2,1,0:T(8,128)}, bf16[32,16,6144]{2,1,0:T(8,128)(2,1)}, f32[8,512]{1,0:T(8,128)}) custom-call(f32[8,208,512]{2,1,0:T(8,128)} %get-tuple-element.60.m_ref, bf16[8,196,512]{2,1,0:T(8,128)(2,1)} %copy.86.ct_ref, f32[8,512]{1,0:T(8,128)} %slice_convert_fusion.vec_ref, ...), custom_call_target="tpu_custom_call" | custom-call | flops 20937965568 | bytes 28934144 | tf_op jit(solution)/shard_map/decoder_mlp/pallas_call | solution.py:243
  263.6 49.4 %decoder_attention_back.1 = (bf16[1024,512]{1,0:T(8,128)(2,1)}, f32[8,512]{1,0:T(8,128)}, bf16[32,16,6144]{2,1,0:T(8,128)(2,1)}) custom-call(s32[1,1024]{1,0:T(1,128)} %compare_select_fusion.key_ref, s32[1024,1]{1,0:T(8,128)} %add_select_fusion.keycol_ref, f32[8,512]{1,0:T(8,128)} %slice_convert_fusion.vec_ref, ...), custom_call_target="tpu_custom_call", output_to_operand_aliasing={{2}: (12, {})} | custom-call | flops 14067695616 | bytes 52772864 | tf_op jit(solution)/shard_map/decoder_attention_back/pallas_call | solution.py:243
  318.0 22.5 %encoder_mlp_back.1 = (bf16[16,48,1664]{2,1,0:T(8,128)(2,1)}, bf16[16,48,1664]{2,1,0:T(8,128)(2,1)}, bf16[16,48,1664]{2,1,0:T(8,128)(2,1)}, bf16[16,48,1664]{2,1...) custom-call(s32[1]{0:T(128)} %bitcast.4.core_ref, bf16[512,512]{1,0:T(8,128)(2,1)} %add_convert_fusion.4.de_ref, ...), custom_call_target="tpu_custom_call" | custom-call | flops 9663676416 | bytes 31244292 | tf_op jit(solution)/shard_map/encoder_mlp_back/pallas_call | solution.py:243
  340.5 14.8 %encoder_attention_back.1 = (bf16[512,768]{1,0:T(8,128)(2,1)}, f32[640,1536]{1,0:T(8,128)}) custom-call(s32[1]{0:T(128)} %bitcast.4.core_ref, f32[512,768]{1,0:T(8,128)} %get-tuple-element.74.dm_ref, bf16[512,768]{1,0:T(8,128)(2,1)} %get-tuple-element.76.q_ref, bf16[640,1536]{1,0:T(8,128)(2,1)} %get-tuple-element.77.kv_ref, ...), custom_call_target="tpu_custom_call" | custom-call | flops 4630511616 | bytes 21266436 | tf_op jit(solution)/shard_map/encoder_attention_back/pallas_call | solution.py:243
  359.0 13.4 %encoder_qkv_back.1 = (bf16[768,1664]{1,0:T(8,128)(2,1)}, bf16[768,1664]{1,0:T(8,128)(2,1)}, f32[512,768]{1,0:T(8,128)}) custom-call(s32[1]{0:T(128)} %bitcast.4.core_ref, bf16[512,768]{1,0:T(8,128)(2,1)} %bitcast.74, f32[512,768]{1,0:T(8,128)} %get-tuple-element.74.dm_ref, bf16[512,768]{1,0:T(8,128)(2,1)} %get-tuple-element.75.o_ref, ...), custom_call_target="tpu_custom_call" | custom-call | flops 4227858432 | bytes 20299780 | tf_op jit(solution)/shard_map/encoder_qkv_back/pallas_call | solution.py:243
  374.0 2.5 slice.231
  385.8 10.5 %collective-permute-done.32 = bf16[4,1,2,48,768]{4,3,2,1,0:T(8,128)(2,1)} collective-permute-done((bf16[4,1,2,48,768]{4,3,2,1,0:T(8,128)(2,1)}, bf16[4,1,2,48,768]{4,3,2,1,0:T(8,128)(2,1)}, u32[]{:S(2)}, u32[]{:S(2)}) %collective-permute-start.32) | collective-permute-done | bytes 589856 | tf_op jit(solution)/shard_map/ppermute | solution.py:109
  400.1 8.6 %collective-permute-done.33 = bf16[4,1,1,48,768]{4,3,2,1,0:T(8,128)(2,1)} collective-permute-done((bf16[4,1,1,48,768]{4,3,2,1,0:T(8,128)(2,1)S(1)}, bf16[4,1,1,48,768]{4,3,2,1,0:T(8,128)(2,1)}, u32[]{:S(2)}, u32[]{:S(2)}) %collective-permute-start.33) | collective-permute-done | bytes 294944 | tf_op jit(solution)/shard_map/ppermute | solution.py:109
  419.3 3.1 collective-permute-done.27
  435.4 3.2 collective-permute-done.30
  438.5 12.2 %collective-permute-done.44 = bf16[4,1,2,48,1664]{4,3,2,1,0:T(8,128)(2,1)S(1)} collective-permute-done((bf16[4,1,2,48,1664]{4,3,2,1,0:T(8,128)(2,1)S(1)}, bf16[4,1,2,48,1664]{4,3,2,1,0:T(8,128)(2,1)S(1)}, u32[]{:S(2)}, u32[]{:S(2)}) %collective-permute-start.44) | collective-permute-done | bytes 1277984 | tf_op jit(solution)/shard_map/ppermute | solution.py:109
  453.2 10.4 %collective-permute-done.38 = bf16[4,2,1,48,1664]{4,3,2,1,0:T(8,128)(2,1)S(1)} collective-permute-done((bf16[4,2,1,48,1664]{4,3,2,1,0:T(8,128)(2,1)S(1)}, bf16[4,2,1,48,1664]{4,3,2,1,0:T(8,128)(2,1)S(1)}, u32[]{:S(2)}, u32[]{:S(2)}) %collective-permute-start.38) | collective-permute-done | bytes 1277984 | tf_op jit(solution)/shard_map/ppermute | solution.py:109
  465.5 11.8 %collective-permute-done.45 = bf16[4,1,1,48,1664]{4,3,2,1,0:T(8,128)(2,1)S(1)} collective-permute-done((bf16[4,1,1,48,1664]{4,3,2,1,0:T(8,128)(2,1)S(1)}, bf16[4,1,1,48,1664]{4,3,2,1,0:T(8,128)(2,1)S(1)}, u32[]{:S(2)}, u32[]{:S(2)}) %collective-permute-start.45) | collective-permute-done | bytes 639008 | tf_op jit(solution)/shard_map/ppermute | solution.py:109
  481.5 3.7 collective-permute-done.46
  489.5 3.2 collective-permute-done.47
  498.0 3.5 collective-permute-done.48
  501.6 2.9 collective-permute-done.42
  512.8 19.1 %reduce-scatter.2.cloned.1.call-done = bf16[16,6144]{1,0:T(8,128)(2,1)} async-done(((bf16[512,6144]{1,0:T(8,128)(2,1)}), bf16[16,6144]{1,0:T(8,128)(2,1)}) %reduce-scatter.2.cloned.1.call-update) | async-done | bytes 196624 | tf_op jit(solution)/shard_map/reduce_scatter | solution.py:1175
  (284 shorter events, 125.3 us)
Async XLA Ops:
  7.2 170.3 %all-gather.2.cloned.1.call-start = ((), (), s32[]{:S(2)}) async-start(), calls=%async_computation.1 | async-start | bytes 6488064 | tf_op jit(solution)/shard_map/all_gather | solution.py:1119
  16.9 514.9 %reduce-scatter.2.cloned.1.call-start = ((), (), s32[]{:S(2)}) async-start(), calls=%async_computation.2 | async-start | bytes 6488064 | tf_op jit(solution)/shard_map/reduce_scatter | solution.py:1175
  17.4 12.8 %collective-permute-start.3 = (bf16[1,1,1,48,1664]{4,3,2,1,0:T(8,128)(2,1)S(1)}, bf16[1,1,1,48,1664]{4,3,2,1,0:T(8,128)(2,1)S(1)}, u32[]{:S(2)}, u32[]{:S(2)}) collective-permute-start(bf16[1,1,1,48,1664]{4,3,2,1,0:T(8,128)(2,1)S(1)} %get-tuple-element.191), channel_id=1, source_target_pairs={{0,16},{2,18},{4,20},{6,22},{8,0},{10,2},{12,4},{14,6},{16,24},{18... | collective-permute-start | bytes 479240 | tf_op jit(solution)/shard_map/ppermute | solution.py:92
  21.5 9.0 %collective-permute-start.9 = (bf16[1,1,1,48,1664]{4,3,2,1,0:T(8,128)(2,1)S(1)}, bf16[1,1,1,48,1664]{4,3,2,1,0:T(8,128)(2,1)S(1)}, u32[]{:S(2)}, u32[]{:S(2)}) collective-permute-start(bf16[1,1,1,48,1664]{4,3,2,1,0:T(8,128)(2,1)S(1)} %get-tuple-element.190), channel_id=1, source_target_pairs={{0,16},{2,18},{4,20},{6,22},{8,0},{10,2},{12,4},{14,6},{16,24},{18... | collective-permute-start | bytes 479240 | tf_op jit(solution)/shard_map/ppermute | solution.py:92
  28.6 16.0 %collective-permute-start.17 = (bf16[1,1,2,48,1664]{4,3,2,1,0:T(8,128)(2,1)S(1)}, bf16[1,1,2,48,1664]{4,3,2,1,0:T(8,128)(2,1)S(1)}, u32[]{:S(2)}, u32[]{:S(2)}) collective-permute-start(bf16[1,1,2,48,1664]{4,3,2,1,0:T(8,128)(2,1)S(1)} %constant_dynamic-update-slice_fusion.31), channel_id=1, source_target_pairs={{0,4},{2,6},{4,0},{6,2},{8,12},{10,14},{12,8},{14,10},{16,20},{18,... | collective-permute-start | bytes 958472 | tf_op jit(solution)/shard_map/ppermute | solution.py:92
  30.2 8.8 %collective-permute-start.4 = (bf16[1,1,1,48,1664]{4,3,2,1,0:T(8,128)(2,1)S(1)}, bf16[1,1,1,48,1664]{4,3,2,1,0:T(8,128)(2,1)S(1)}, u32[]{:S(2)}, u32[]{:S(2)}) collective-permute-start(bf16[1,1,1,48,1664]{4,3,2,1,0:T(8,128)(2,1)S(1)} %collective-permute-done.3), channel_id=1, source_target_pairs={{0,16},{2,18},{4,20},{6,22},{8,0},{10,2},{12,4},{14,6},{16,24},{18... | collective-permute-start | bytes 479240 | tf_op jit(solution)/shard_map/ppermute | solution.py:92
  30.5 13.1 %collective-permute-start.10 = (bf16[1,1,1,48,1664]{4,3,2,1,0:T(8,128)(2,1)S(1)}, bf16[1,1,1,48,1664]{4,3,2,1,0:T(8,128)(2,1)S(1)}, u32[]{:S(2)}, u32[]{:S(2)}) collective-permute-start(bf16[1,1,1,48,1664]{4,3,2,1,0:T(8,128)(2,1)S(1)} %collective-permute-done.9), channel_id=1, source_target_pairs={{0,16},{2,18},{4,20},{6,22},{8,0},{10,2},{12,4},{14,6},{16,24},{18... | collective-permute-start | bytes 479240 | tf_op jit(solution)/shard_map/ppermute | solution.py:92
  44.6 25.2 %collective-permute-start.18 = (bf16[1,2,2,48,1664]{4,3,2,1,0:T(8,128)(2,1)S(1)}, bf16[1,2,2,48,1664]{4,3,2,1,0:T(8,128)(2,1)S(1)}, u32[]{:S(2)}, u32[]{:S(2)}) collective-permute-start(bf16[1,2,2,48,1664]{4,3,2,1,0:T(8,128)(2,1)S(1)} %constant_dynamic-update-slice_fusion.29), channel_id=1, source_target_pairs={{0,16},{2,18},{4,20},{6,22},{8,0},{10,2},{12,4},{14,6},{16,24},{18... | collective-permute-start | bytes 1916936 | tf_op jit(solution)/shard_map/ppermute | solution.py:92
  47.4 12.6 %collective-permute-start.6 = (bf16[4,1,1,48,1664]{4,3,2,1,0:T(8,128)(2,1)S(1)}, bf16[4,1,1,48,1664]{4,3,2,1,0:T(8,128)(2,1)S(1)}, u32[]{:S(2)}, u32[]{:S(2)}) collective-permute-start(bf16[4,1,1,48,1664]{4,3,2,1,0:T(8,128)(2,1)S(1)} %constant_dynamic-update-slice_fusion.45), channel_id=1, source_target_pairs={{0,2},{2,0},{4,6},{6,4},{8,10},{10,8},{12,14},{14,12},{16,18},{18,... | collective-permute-start | bytes 1916936 | tf_op jit(solution)/shard_map/ppermute | solution.py:92
  51.5 17.4 %collective-permute-start.12 = (bf16[4,1,1,48,1664]{4,3,2,1,0:T(8,128)(2,1)S(1)}, bf16[4,1,1,48,1664]{4,3,2,1,0:T(8,128)(2,1)S(1)}, u32[]{:S(2)}, u32[]{:S(2)}) collective-permute-start(bf16[4,1,1,48,1664]{4,3,2,1,0:T(8,128)(2,1)S(1)} %constant_dynamic-update-slice_fusion.37), channel_id=1, source_target_pairs={{0,4},{2,6},{4,0},{6,2},{8,12},{10,14},{12,8},{14,10},{16,20},{18,... | collective-permute-start | bytes 1916936 | tf_op jit(solution)/shard_map/ppermute | solution.py:92
  60.1 34.1 %collective-permute-start.7 = (bf16[4,1,2,48,1664]{4,3,2,1,0:T(8,128)(2,1)S(1)}, bf16[4,1,2,48,1664]{4,3,2,1,0:T(8,128)(2,1)S(1)}, u32[]{:S(2)}, u32[]{:S(2)}) collective-permute-start(bf16[4,1,2,48,1664]{4,3,2,1,0:T(8,128)(2,1)S(1)} %constant_dynamic-update-slice_fusion.43), channel_id=1, source_target_pairs={{0,4},{2,6},{4,0},{6,2},{8,12},{10,14},{12,8},{14,10},{16,20},{18,... | collective-permute-start | bytes 3833864 | tf_op jit(solution)/shard_map/ppermute | solution.py:92
  68.9 25.9 %collective-permute-start.13 = (bf16[4,2,1,48,1664]{4,3,2,1,0:T(8,128)(2,1)S(1)}, bf16[4,2,1,48,1664]{4,3,2,1,0:T(8,128)(2,1)S(1)}, u32[]{:S(2)}, u32[]{:S(2)}) collective-permute-start(bf16[4,2,1,48,1664]{4,3,2,1,0:T(8,128)(2,1)S(1)} %constant_dynamic-update-slice_fusion.35), channel_id=1, source_target_pairs={{0,2},{2,0},{4,6},{6,4},{8,10},{10,8},{12,14},{14,12},{16,18},{18,... | collective-permute-start | bytes 3833864 | tf_op jit(solution)/shard_map/ppermute | solution.py:92
  69.8 23.3 %collective-permute-start.19 = (bf16[1,2,2,48,1664]{4,3,2,1,0:T(8,128)(2,1)S(1)}, bf16[1,2,2,48,1664]{4,3,2,1,0:T(8,128)(2,1)S(1)}, u32[]{:S(2)}, u32[]{:S(2)}) collective-permute-start(bf16[1,2,2,48,1664]{4,3,2,1,0:T(8,128)(2,1)S(1)} %collective-permute-done.18), channel_id=1, source_target_pairs={{0,16},{2,18},{4,20},{6,22},{8,0},{10,2},{12,4},{14,6},{16,24},{18... | collective-permute-start | bytes 1916936 | tf_op jit(solution)/shard_map/ppermute | solution.py:92
  93.1 25.6 %collective-permute-start.20 = (bf16[1,2,2,48,1664]{4,3,2,1,0:T(8,128)(2,1)S(1)}, bf16[1,2,2,48,1664]{4,3,2,1,0:T(8,128)(2,1)S(1)}, u32[]{:S(2)}, u32[]{:S(2)}) collective-permute-start(bf16[1,2,2,48,1664]{4,3,2,1,0:T(8,128)(2,1)S(1)} %collective-permute-done.19), channel_id=1, source_target_pairs={{0,16},{2,18},{4,20},{6,22},{8,0},{10,2},{12,4},{14,6},{16,24},{18... | collective-permute-start | bytes 1916936 | tf_op jit(solution)/shard_map/ppermute | solution.py:92
  94.4 39.1 %collective-permute-start.8 = (bf16[16,48,1664]{2,1,0:T(8,128)(2,1)S(1)}, bf16[16,48,1664]{2,1,0:T(8,128)(2,1)}, u32[]{:S(2)}, u32[]{:S(2)}) collective-permute-start(bf16[16,48,1664]{2,1,0:T(8,128)(2,1)S(1)} %bitcast.64), channel_id=1, source_target_pairs={{0,1},{1,0},{2,3},{3,2},{4,5},{5,4},{6,7},{7,6},{8,9},{9,8},{10,11... | collective-permute-start | bytes 7667720 | tf_op jit(solution)/shard_map/ppermute | solution.py:1130
  96.2 58.1 %collective-permute-start.14 = (bf16[16,48,1664]{2,1,0:T(8,128)(2,1)}, bf16[16,48,1664]{2,1,0:T(8,128)(2,1)}, u32[]{:S(2)}, u32[]{:S(2)}) collective-permute-start(bf16[16,48,1664]{2,1,0:T(8,128)(2,1)} %bitcast.22.mu_ref), channel_id=1, source_target_pairs={{0,1},{1,0},{2,3},{3,2},{4,5},{5,4},{6,7},{7,6},{8,9},{9,8},{10,11... | collective-permute-start | bytes 7667720 | tf_op jit(solution)/shard_map/ppermute | solution.py:1130
  119.6 34.7 %collective-permute-start.21 = (bf16[16,48,1664]{2,1,0:T(8,128)(2,1)}, bf16[16,48,1664]{2,1,0:T(8,128)(2,1)}, u32[]{:S(2)}, u32[]{:S(2)}) collective-permute-start(bf16[16,48,1664]{2,1,0:T(8,128)(2,1)} %bitcast.24.md_ref), channel_id=1, source_target_pairs={{0,1},{1,0},{2,3},{3,2},{4,5},{5,4},{6,7},{7,6},{8,9},{9,8},{10,11... | collective-permute-start | bytes 7667720 | tf_op jit(solution)/shard_map/ppermute | solution.py:1130
  119.6 8.7 %collective-permute-start = (s32[512]{0:T(512)S(1)}, s32[512]{0:T(512)S(1)}, u32[]{:S(2)}, u32[]{:S(2)}) collective-permute-start(s32[512]{0:T(512)S(1)} %bitcast.85), channel_id=1, source_target_pairs={{0,1},{1,0},{2,3},{3,2},{4,5},{5,4},{6,7},{7,6},{8,9},{9,8},{10,11... | collective-permute-start | bytes 6152 | tf_op jit(solution)/shard_map/ppermute | solution.py:1140
  121.0 11.3 %collective-permute-start.1 = (bf16[128,768]{1,0:T(8,128)(2,1)S(1)}, bf16[128,768]{1,0:T(8,128)(2,1)S(1)}, u32[]{:S(2)}, u32[]{:S(2)}) collective-permute-start(bf16[128,768]{1,0:T(8,128)(2,1)S(1)} %dynamic-slice_bitcast_fusion), channel_id=1, source_target_pairs={{0,1},{1,0},{2,3},{3,2},{4,5},{5,4},{6,7},{7,6},{8,9},{9,8},{10,11... | collective-permute-start | bytes 589832 | tf_op jit(solution)/shard_map/ppermute | solution.py:1154
  376.9 38.4 %collective-permute-start.43 = (bf16[16,48,1664]{2,1,0:T(8,128)(2,1)}, bf16[16,48,1664]{2,1,0:T(8,128)(2,1)}, u32[]{:S(2)}, u32[]{:S(2)}) collective-permute-start(bf16[16,48,1664]{2,1,0:T(8,128)(2,1)} %get-tuple-element.92), channel_id=1, source_target_pairs={{0,1},{1,0},{2,3},{3,2},{4,5},{5,4},{6,7},{7,6},{8,9},{9,8},{10,11... | collective-permute-start | bytes 7667720 | tf_op jit(solution)/shard_map/ppermute | solution.py:1190
  380.4 15.9 %collective-permute-start.32 = (bf16[4,1,2,48,768]{4,3,2,1,0:T(8,128)(2,1)}, bf16[4,1,2,48,768]{4,3,2,1,0:T(8,128)(2,1)}, u32[]{:S(2)}, u32[]{:S(2)}) collective-permute-start(bf16[4,1,2,48,768]{4,3,2,1,0:T(8,128)(2,1)} %add_convert_fusion.3), channel_id=1, source_target_pairs={{0,4},{2,6},{4,0},{6,2},{8,12},{10,14},{12,8},{14,10},{16,20},{18,... | collective-permute-start | bytes 1769480 | tf_op jit(solution)/shard_map/ppermute | solution.py:109
  380.4 43.2 %collective-permute-start.37 = (bf16[16,48,1664]{2,1,0:T(8,128)(2,1)}, bf16[16,48,1664]{2,1,0:T(8,128)(2,1)}, u32[]{:S(2)}, u32[]{:S(2)}) collective-permute-start(bf16[16,48,1664]{2,1,0:T(8,128)(2,1)} %get-tuple-element.90), channel_id=1, source_target_pairs={{0,1},{1,0},{2,3},{3,2},{4,5},{5,4},{6,7},{7,6},{8,9},{9,8},{10,11... | collective-permute-start | bytes 7667720 | tf_op jit(solution)/shard_map/ppermute | solution.py:1190
  384.5 25.2 %collective-permute-start.26 = (bf16[4,2,1,48,896]{4,3,2,1,0:T(8,128)(2,1)}, bf16[4,2,1,48,896]{4,3,2,1,0:T(8,128)(2,1)S(1)}, u32[]{:S(2)}, u32[]{:S(2)}) collective-permute-start(bf16[4,2,1,48,896]{4,3,2,1,0:T(8,128)(2,1)} %add_convert_fusion.2), channel_id=1, source_target_pairs={{0,2},{2,0},{4,6},{6,4},{8,10},{10,8},{12,14},{14,12},{16,18},{18,... | collective-permute-start | bytes 2064392 | tf_op jit(solution)/shard_map/ppermute | solution.py:109
  398.7 9.9 %collective-permute-start.33 = (bf16[4,1,1,48,768]{4,3,2,1,0:T(8,128)(2,1)S(1)}, bf16[4,1,1,48,768]{4,3,2,1,0:T(8,128)(2,1)}, u32[]{:S(2)}, u32[]{:S(2)}) collective-permute-start(bf16[4,1,1,48,768]{4,3,2,1,0:T(8,128)(2,1)S(1)} %dynamic-slice_convert_fusion.4), channel_id=1, source_target_pairs={{0,2},{2,0},{4,6},{6,4},{8,10},{10,8},{12,14},{14,12},{16,18},{18,... | collective-permute-start | bytes 884744 | tf_op jit(solution)/shard_map/ppermute | solution.py:109
  411.4 11.0 %collective-permute-start.27 = (bf16[4,1,1,48,896]{4,3,2,1,0:T(8,128)(2,1)S(1)}, bf16[4,1,1,48,896]{4,3,2,1,0:T(8,128)(2,1)S(1)}, u32[]{:S(2)}, u32[]{:S(2)}) collective-permute-start(bf16[4,1,1,48,896]{4,3,2,1,0:T(8,128)(2,1)S(1)} %dynamic-slice_convert_fusion.3), channel_id=1, source_target_pairs={{0,4},{2,6},{4,0},{6,2},{8,12},{10,14},{12,8},{14,10},{16,20},{18,... | collective-permute-start | bytes 1032200 | tf_op jit(solution)/shard_map/ppermute | solution.py:109
  414.1 15.3 %collective-permute-start.35 = (bf16[1,1,1,48,768]{4,3,2,1,0:T(8,128)(2,1)S(1)}, bf16[1,1,1,48,768]{4,3,2,1,0:T(8,128)(2,1)S(1)}, u32[]{:S(2)}, u32[]{:S(2)}) collective-permute-start(bf16[1,1,1,48,768]{4,3,2,1,0:T(8,128)(2,1)S(1)} %add_convert_fusion.12), channel_id=1, source_target_pairs={{0,16},{2,18},{4,20},{6,22},{8,0},{10,2},{12,4},{14,6},{16,24},{18... | collective-permute-start | bytes 221192 | tf_op jit(solution)/shard_map/ppermute | solution.py:109
  417.2 33.5 %collective-permute-start.44 = (bf16[4,1,2,48,1664]{4,3,2,1,0:T(8,128)(2,1)S(1)}, bf16[4,1,2,48,1664]{4,3,2,1,0:T(8,128)(2,1)S(1)}, u32[]{:S(2)}, u32[]{:S(2)}) collective-permute-start(bf16[4,1,2,48,1664]{4,3,2,1,0:T(8,128)(2,1)S(1)} %add_convert_fusion), channel_id=1, source_target_pairs={{0,4},{2,6},{4,0},{6,2},{8,12},{10,14},{12,8},{14,10},{16,20},{18,... | collective-permute-start | bytes 3833864 | tf_op jit(solution)/shard_map/ppermute | solution.py:109
  425.3 38.2 %collective-permute-start.38 = (bf16[4,2,1,48,1664]{4,3,2,1,0:T(8,128)(2,1)S(1)}, bf16[4,2,1,48,1664]{4,3,2,1,0:T(8,128)(2,1)S(1)}, u32[]{:S(2)}, u32[]{:S(2)}) collective-permute-start(bf16[4,2,1,48,1664]{4,3,2,1,0:T(8,128)(2,1)S(1)} %add_convert_fusion.1), channel_id=1, source_target_pairs={{0,2},{2,0},{4,6},{6,4},{8,10},{10,8},{12,14},{14,12},{16,18},{18,... | collective-permute-start | bytes 3833864 | tf_op jit(solution)/shard_map/ppermute | solution.py:109
  452.6 24.7 %collective-permute-start.45 = (bf16[4,1,1,48,1664]{4,3,2,1,0:T(8,128)(2,1)S(1)}, bf16[4,1,1,48,1664]{4,3,2,1,0:T(8,128)(2,1)S(1)}, u32[]{:S(2)}, u32[]{:S(2)}) collective-permute-start(bf16[4,1,1,48,1664]{4,3,2,1,0:T(8,128)(2,1)S(1)} %dynamic-slice_convert_fusion), channel_id=1, source_target_pairs={{0,2},{2,0},{4,6},{6,4},{8,10},{10,8},{12,14},{14,12},{16,18},{18,... | collective-permute-start | bytes 1916936 | tf_op jit(solution)/shard_map/ppermute | solution.py:109
  465.4 14.1 %collective-permute-start.39 = (bf16[4,1,1,48,1664]{4,3,2,1,0:T(8,128)(2,1)S(1)}, bf16[4,1,1,48,1664]{4,3,2,1,0:T(8,128)(2,1)S(1)}, u32[]{:S(2)}, u32[]{:S(2)}) collective-permute-start(bf16[4,1,1,48,1664]{4,3,2,1,0:T(8,128)(2,1)S(1)} %dynamic-slice_convert_fusion.1), channel_id=1, source_target_pairs={{0,4},{2,6},{4,0},{6,2},{8,12},{10,14},{12,8},{14,10},{16,20},{18,... | collective-permute-start | bytes 1916936 | tf_op jit(solution)/shard_map/ppermute | solution.py:109
  479.7 8.9 %collective-permute-start.40 = (bf16[1,1,1,48,1664]{4,3,2,1,0:T(8,128)(2,1)S(1)}, bf16[1,1,1,48,1664]{4,3,2,1,0:T(8,128)(2,1)S(1)}, u32[]{:S(2)}, u32[]{:S(2)}) collective-permute-start(bf16[1,1,1,48,1664]{4,3,2,1,0:T(8,128)(2,1)S(1)} %dynamic-slice_convert_fusion.6), channel_id=1, source_target_pairs={{0,16},{2,18},{4,20},{6,22},{8,0},{10,2},{12,4},{14,6},{16,24},{18... | collective-permute-start | bytes 479240 | tf_op jit(solution)/shard_map/ppermute | solution.py:109
  492.7 8.8 %collective-permute-start.48 = (bf16[1,1,1,48,1664]{4,3,2,1,0:T(8,128)(2,1)S(1)}, bf16[1,1,1,48,1664]{4,3,2,1,0:T(8,128)(2,1)S(1)}, u32[]{:S(2)}, u32[]{:S(2)}) collective-permute-start(bf16[1,1,1,48,1664]{4,3,2,1,0:T(8,128)(2,1)S(1)} %add_convert_fusion.5), channel_id=1, source_target_pairs={{0,16},{2,18},{4,20},{6,22},{8,0},{10,2},{12,4},{14,6},{16,24},{18... | collective-permute-start | bytes 479240 | tf_op jit(solution)/shard_map/ppermute | solution.py:109
  (37 other events, 322.5 us)
Sparse Core Ops, SparseCore 0:
  17.1 108.1 all-gather.1
  400.2 131.5 reduce-scatter.1
